TPU v7x, 256 devices: a whole 4x4x8 slice. The times are simulated.
256 devices in a mesh: dp: 128 (over z, y, x), tensor: 2 (over core).
Axes of the slice: x: 4, y: 4, z: 8, core: 2. Of those that a mesh axis runs over, the one named last changes fastest.
Arguments:
- x_saved: bfloat16 [2, 32768, 7168], P(None, ('dp', 'tensor')), may hold values from -6 to 6
- grad_pre: bfloat16 [2, 32768, 10240], P(None, 'dp', 'tensor'), may hold values from -6 to 6
- q_prev: float32 [2, 10240, 64], P(None, 'tensor'), may hold values from -6 to 6
Outputs:
- p_hat: float32 [2, 7168, 64], P(None, 'tensor')
- q_new: float32 [2, 10240, 64], P(None, 'tensor')
All inputs are finite; a program needn't handle non-finite values.
Results may differ from a plain program's by a relative error of at most 0.018.
Values may be sent and summed in bfloat16 or wider, within the bound.
No kernel may reach another device: no remote copies, remote signals or barrier semaphores. Data moves between devices by JAX's collectives and lax.ppermute only.
A program may use at most 128 MiB of HBM per device.

v0:
```python
import jax
import jax.numpy as jnp
from jax import lax
from jax.sharding import PartitionSpec as P


def gram_of(rows):
    return jnp.einsum("ldr,lds->lrs", rows, rows, precision=lax.Precision.HIGHEST)


def normalize(rows, gram_matrix):
    lower_factor = jnp.linalg.cholesky(gram_matrix)
    return lax.linalg.triangular_solve(
        lower_factor, rows, left_side=False, lower=True, transpose_a=True
    )


def compress(x_saved, grad_pre, q_prev):
    tok_total = grad_pre.shape[1] * lax.axis_size("dp")
    norm_scale = float(tok_total) ** (-0.5)
    half_q = q_prev.astype(jnp.bfloat16)
    partial_value = jnp.einsum(
        "ltf,lfr->ltr", grad_pre, half_q, preferred_element_type=jnp.float32
    ).astype(jnp.bfloat16)
    full_x = lax.all_gather(x_saved, "tensor", axis=1, tiled=True)
    p_part = jnp.einsum("ltd,ltr->ldr", full_x, partial_value, preferred_element_type=jnp.float32)
    p_rows = lax.psum_scatter(
        p_part.astype(jnp.bfloat16), "tensor", scatter_dimension=1, tiled=True
    ).astype(jnp.float32)
    p_rows = lax.psum(p_rows, "dp")
    gram_matrix = lax.psum(gram_of(p_rows).astype(jnp.bfloat16), "tensor").astype(jnp.float32)
    p_hat = normalize(p_rows, gram_matrix)
    p_full = lax.all_gather(p_hat.astype(jnp.bfloat16), "tensor", axis=1, tiled=True)
    proj = jnp.einsum("ltd,ldr->ltr", full_x, p_full, preferred_element_type=jnp.float32).astype(
        jnp.bfloat16
    )
    q_part = jnp.einsum("ltf,ltr->lfr", grad_pre, proj, preferred_element_type=jnp.float32)
    q_new = lax.psum(q_part * norm_scale, "dp")
    return (p_hat, q_new)


def on_device(x_saved, grad_pre, q_prev):
    hat_list = []
    new_list = []
    for layer_index in range(x_saved.shape[0]):
        p_hat, q_new = compress(
            x_saved[layer_index : layer_index + 1],
            grad_pre[layer_index : layer_index + 1],
            q_prev[layer_index : layer_index + 1],
        )
        hat_list.append(p_hat)
        new_list.append(q_new)
    return (jnp.concatenate(hat_list, axis=0), jnp.concatenate(new_list, axis=0))


def solution(mesh):
    placed = (P(None, ("dp", "tensor"), None), P(None, "dp", "tensor"), P(None, "tensor", None))
    return jax.shard_map(
        on_device,
        mesh=mesh,
        in_specs=placed,
        out_specs=(P(None, "tensor", None), P(None, "tensor", None)),
        check_vma=False,
    )
```

profile of v0, /device:TPU:8, one launch (start us, length us, event | category | flops | bytes accessed | tf_op | source)
XLA Modules:
  0.0 1080.5 jit_solution(260368601308259915)
XLA Ops:
  7.2 4.1 fusion.58
  11.4 0.7 all-gather.5.cloned.1.call-update
  12.2 1.9 convert.4
  14.1 18.6 %all-gather.3.cloned.1.call-done = bf16[1,256,7168]{2,1,0:T(8,128)(2,1)} async-done(((bf16[1,128,7168]{2,1,0:T(8,128)(2,1)}), bf16[1,256,7168]{2,1,0:T(8,128)(2,1)}) %all-gather.3.cloned.1.call-update) | async-done | bytes 3670032 | tf_op jit(solution)/shard_map/all_gather | solution.py:25
  32.6 6.2 fusion
  38.9 15.6 %all-gather.5.cloned.1.call-done = bf16[1,256,7168]{2,1,0:T(8,128)(2,1)} async-done(((bf16[1,128,7168]{2,1,0:T(8,128)(2,1)}), bf16[1,256,7168]{2,1,0:T(8,128)(2,1)}) %all-gather.5.cloned.1.call-update) | async-done | bytes 3670032 | tf_op jit(solution)/shard_map/all_gather | solution.py:25
  54.6 6.2 fusion.1
  60.8 11.2 %reduce-scatter.3.cloned.1.call-done = bf16[1,3584,64]{1,2,0:T(8,128)(2,1)} async-done(((bf16[1,7168,64]{1,2,0:T(8,128)(2,1)}), bf16[1,3584,64]{1,2,0:T(8,128)(2,1)}) %reduce-scatter.3.cloned.1.call-update) | async-done | bytes 458768 | tf_op jit(solution)/shard_map/reduce_scatter | solution.py:27
  72.1 18.2 %reduce-scatter.5.cloned.1.call-done = bf16[1,3584,64]{1,2,0:T(8,128)(2,1)} async-done(((bf16[1,7168,64]{1,2,0:T(8,128)(2,1)}), bf16[1,3584,64]{1,2,0:T(8,128)(2,1)}) %reduce-scatter.5.cloned.1.call-update) | async-done | bytes 458768 | tf_op jit(solution)/shard_map/reduce_scatter | solution.py:27
  90.2 697.3 %all-reduce.7 = (f32[1,3584,64]{1,2,0:T(8,128)S(1)}, f32[1,3584,64]{1,2,0:T(8,128)S(1)}) all-reduce(bf16[1,3584,64]{1,2,0:T(8,128)(2,1)} %reduce-scatter.5.cloned.1.call-done, bf16[1,3584,64]{1,2,0:T(8,128)(2,1)} %reduce-scatter.3.cloned.1.call-done), channel_id=1, replica_groups=mesh['dp'=128,'tensor'=2] {'dp'}, use_global_device_ids=true, to_apply=%region_6.9 | all-reduce | flops 458752 | bytes 2752512 | tf_op jit(solution)/shard_map/psum | solution.py:30
  787.5 0.9 fusion.32
  788.4 0.9 fusion.33
  789.3 3.4 all-reduce.2
  792.8 0.1 copy.8
  792.9 5.8 custom-call.8
  798.8 0.6 compare_reduce_fusion.1
  799.4 0.7 fusion.52
  800.1 4.9 custom-call.9
  805.0 0.9 fusion.60
  805.9 2.6 all_gather.14
  808.6 5.8 custom-call.10
  814.4 0.6 compare_reduce_fusion
  815.1 0.7 fusion.53
  815.7 4.9 custom-call.11
  820.6 1.9 fusion.59
  822.5 2.4 all_gather.15
  825.0 6.2 fusion.3
  831.2 6.2 fusion.2
  837.4 1.2 copy-done
  838.5 1.4 pad_maximum_fusion.1
  839.9 230.6 %all-reduce.6.cloned.1.call-done = (f32[1,5120,64]{1,2,0:T(8,128)}, f32[1,5120,64]{1,2,0:T(8,128)}) async-done(((f32[1,5120,64]{1,2,0:T(8,128)}, f32[1,5120,64]{1,2,0:T(8,128)}), (f32[1,5120,64]{1,2,0:T(8,128)}, f32[1,5120,64]{1,2,0:T(8,128)})) %all-reduce.6.cloned.1.call-update) | async-done | bytes 2621456 | tf_op jit(solution)/shard_map/psum | solution.py:38
  1070.5 3.5 pad_maximum_fusion
  (14 shorter events, 0.4 us)
Async XLA Ops:
  7.2 25.5 %all-gather.3.cloned.1.call-start = ((), (), s32[]{:S(2)}) async-start(), calls=%async_computation.2 | async-start | bytes 5505024 | tf_op jit(solution)/shard_map/all_gather | solution.py:25
  11.4 43.2 %all-gather.5.cloned.1.call-start = ((), (), s32[]{:S(2)}) async-start(), calls=%async_computation.4 | async-start | bytes 5505024 | tf_op jit(solution)/shard_map/all_gather | solution.py:25
  12.1 60.0 %reduce-scatter.3.cloned.1.call-start = ((), (), s32[]{:S(2)}) async-start(), calls=%async_computation.3 | async-start | bytes 1376256 | tf_op jit(solution)/shard_map/reduce_scatter | solution.py:27
  38.9 51.4 %reduce-scatter.5.cloned.1.call-start = ((), (), s32[]{:S(2)}) async-start(), calls=%async_computation.5 | async-start | bytes 1376256 | tf_op jit(solution)/shard_map/reduce_scatter | solution.py:27
  60.8 1009.7 %all-reduce.6.cloned.1.call-start = ((), (), s32[]{:S(2)}) async-start(), calls=%async_computation.6 | async-start | bytes 5242880 | tf_op jit(solution)/shard_map/psum | solution.py:38
  837.3 1.2 copy-start
Sparse Core Ops, SparseCore 0:
  11.5 21.1 all-gather.2
  35.0 19.5 all-gather.4
  57.1 14.9 reduce-scatter.2
  75.2 15.0 reduce-scatter.4
  837.5 232.9 all-reduce.5
where the time goes:
time: 1080 us
  blocking collectives  706 us (65%)
  waiting for transfers between devices  295 us (27%)
  other arithmetic  30.9 us (3%)
  matrix products  29.4 us (3%)
  between operations  13.9 us (1%)
    psum x1, blocking collectives, compress(): p_rows = lax.psum(p_rows, 'dp')  697 us
    psum x1, waiting for transfers between devices, compress(): q_new = lax.psum(q_part * norm_scale, 'dp')  231 us
    all_gather x2, waiting for transfers between devices, compress(): full_x = lax.all_gather(x_saved, 'tensor', axis=1, tiled=True)  34.2 us
    reduce_scatter x2, waiting for transfers between devices, compress(): lax.psum_scatter(p_part.astype(jnp.bfloat16), 'tensor', scatter_dimension...  29.4 us
  transfers between devices with their start and end apart: 5, of which 5 were waited for; matrix products, arithmetic and copies ran while one was open for 1% of the time, Pallas kernels for 0%

commit v1 on v0

v1 whole, which is shorter than its diff:
```python
import jax
import jax.numpy as jnp
from jax import lax
from jax.experimental import pallas as pl
from jax.experimental.pallas import tpu as pltpu
from jax.sharding import Mesh
from jax.sharding import PartitionSpec as P

LANES = 128
NEAR = ("zl", "x", "y")
FAR = ("zh",)
CHIPS = ("zh", "zl", "y", "x")
CORE = "core"
F32, BF16 = jnp.float32, jnp.bfloat16
TRANSPOSED = (((1,), (1,)), ((), ()))


def params(mib):
    return pltpu.CompilerParams(vmem_limit_bytes=mib << 20)


def swap(value):
    return lax.ppermute(value, CORE, [(0, 1), (1, 0)])


def partial_body(grad_ref, q_ref, out_ref, total):
    step = pl.program_id(1)

    @pl.when(step == 0)
    def _():
        total[...] = jnp.zeros_like(total)

    total[...] += lax.dot_general(
        q_ref[0].astype(BF16), grad_ref[0], TRANSPOSED, preferred_element_type=F32
    )

    @pl.when(step == pl.num_programs(1) - 1)
    def _():
        out_ref[0] = total[...].astype(BF16)


def partial_of(grad, q_rows):
    layers, tokens, hidden = grad.shape
    rank = q_rows.shape[1]
    steps = 4
    block = hidden // steps
    return pl.pallas_call(
        partial_body,
        grid=(layers, steps),
        in_specs=[
            pl.BlockSpec((1, tokens, block), lambda l, k: (l, 0, k)),
            pl.BlockSpec((1, rank, block), lambda l, k: (l, 0, k)),
        ],
        out_specs=pl.BlockSpec((1, rank, tokens), lambda l, k: (l, 0, 0)),
        out_shape=jax.ShapeDtypeStruct((layers, rank, tokens), BF16),
        scratch_shapes=[pltpu.VMEM((rank, tokens), F32)],
        compiler_params=params(24),
        name="partial",
    )(grad, q_rows)


def own_first(core, value):
    mid = value.shape[1] // 2
    low, high = value[:, :mid], value[:, mid:]
    return jnp.concatenate(
        [jnp.where(core == 0, low, high), jnp.where(core == 0, high, low)], axis=1
    )


def left_body(core_ref, own_ref, in_ref, mine_ref, theirs_ref, out_ref):
    core = core_ref[0]
    rank = mine_ref.shape[1]
    both = jnp.concatenate(
        [own_first(core, mine_ref[0].astype(F32)), own_first(core, theirs_ref[0].astype(F32))], axis=0
    ).astype(BF16)
    wide = 2 * LANES
    for tile in range(own_ref.shape[2] // wide):
        at = slice(tile * wide, (tile + 1) * wide)
        rows = jnp.concatenate([own_ref[0, :, at], in_ref[0, :, at]], axis=0)
        got = jnp.dot(both, rows, preferred_element_type=F32)
        got = (got[:rank] + got[rank:]).astype(BF16)
        out_ref[0, 2 * tile] = got[:, :LANES]
        out_ref[0, 2 * tile + 1] = got[:, LANES:]


def left_of(core, x_own, x_in, mine, theirs):
    layers, tokens, half = x_in.shape
    rank = mine.shape[1]
    steps = 2
    block = half // steps
    tiles = block // LANES
    return pl.pallas_call(
        left_body,
        grid_spec=pltpu.PrefetchScalarGridSpec(
            num_scalar_prefetch=1,
            grid=(layers, steps),
            in_specs=[
                pl.BlockSpec((1, tokens, block), lambda l, k, c: (l, 0, c[0] * steps + k)),
                pl.BlockSpec((1, tokens, block), lambda l, k, c: (l, 0, k)),
                pl.BlockSpec((1, rank, 2 * tokens), lambda l, k, c: (l, 0, 0)),
                pl.BlockSpec((1, rank, 2 * tokens), lambda l, k, c: (l, 0, 0)),
            ],
            out_specs=pl.BlockSpec((1, tiles, rank, LANES), lambda l, k, c: (l, k, 0, 0)),
        ),
        out_shape=jax.ShapeDtypeStruct((layers, half // LANES, rank, LANES), BF16),
        compiler_params=params(24),
        name="left",
    )(core, x_own, x_in, mine, theirs)


def inner_body(core_ref, own_ref, in_ref, p_ref, out_ref):
    core = core_ref[0]
    layers, tiles, rank = p_ref.shape[:3]
    tokens = 2 * own_ref.shape[1]
    parts, grams = [], []
    for layer in range(layers):
        rows = jnp.concatenate([p_ref[layer, tile] for tile in range(tiles)], axis=1)
        seen = jnp.concatenate([own_ref[layer], in_ref[layer]], axis=0)
        got = lax.dot_general(rows, seen, TRANSPOSED, preferred_element_type=F32)
        parts.append(own_first(core, got))
        grams.append(lax.dot_general(rows, rows, TRANSPOSED, preferred_element_type=F32))
    value = jnp.concatenate(parts + grams, axis=1)

    @pl.when(pl.program_id(0) == 0)
    def _():
        out_ref[...] = value

    @pl.when(pl.program_id(0) > 0)
    def _():
        out_ref[...] += value


def inner_of(core, x_own, x_in, p_blocks):
    layers, tokens, half = x_in.shape
    rank = p_blocks.shape[2]
    steps = 2
    block = half // steps
    tiles = block // LANES
    width = layers * (2 * tokens + rank)
    return pl.pallas_call(
        inner_body,
        grid_spec=pltpu.PrefetchScalarGridSpec(
            num_scalar_prefetch=1,
            grid=(steps,),
            in_specs=[
                pl.BlockSpec((layers, tokens, block), lambda k, c: (0, 0, c[0] * steps + k)),
                pl.BlockSpec((layers, tokens, block), lambda k, c: (0, 0, k)),
                pl.BlockSpec((layers, tiles, rank, LANES), lambda k, c: (0, k, 0, 0)),
            ],
            out_specs=pl.BlockSpec((rank, width), lambda k, c: (0, 0)),
        ),
        out_shape=jax.ShapeDtypeStruct((rank, width), F32),
        compiler_params=params(24),
        name="inner",
    )(core, x_own, x_in, p_blocks)


def inverse_factors(grams, store):
    rank = grams[0].shape[0]
    height = 8
    blocks = rank // height
    line = lax.broadcasted_iota(jnp.int32, (height, rank), 0)
    column = lax.broadcasted_iota(jnp.int32, (height, rank), 1)
    row_id = lax.broadcasted_iota(jnp.int32, (height, 1), 0)
    state = []
    for gram in grams:
        state.append([
            jnp.concatenate(
                [
                    gram[b * height : (b + 1) * height],
                    jnp.where(column == line + b * height, 1.0, 0.0).astype(F32),
                ],
                axis=1,
            )
            for b in range(blocks)
        ])
    for j in range(rank):
        at, low = j // height, j % height
        for index, rows in enumerate(state):
            pivot_row = rows[at][low : low + 1]
            root = lax.rsqrt(pivot_row[:, j : j + 1])
            scaled = pivot_row * root
            store(index, j, scaled[:, rank:])
            for b in range(at, blocks):
                if b == at and low == height - 1:
                    continue
                factor = rows[b][:, j : j + 1] * root
                if b == at:
                    factor = jnp.where(row_id > low, factor, 0.0)
                rows[b] = rows[b] - factor * scaled


def split3(value):
    high = value.astype(BF16)
    rest = value - high.astype(F32)
    mid = rest.astype(BF16)
    return high, mid, (rest - mid.astype(F32)).astype(BF16)


def right_body(scale, mine_ref, theirs_ref, grad_ref, inverse_ref, out_ref, proj):
    layers, rank, tokens = proj.shape

    @pl.when((pl.program_id(0) == 0) & (pl.program_id(1) == 0))
    def _():
        total = mine_ref[...] + theirs_ref[...]
        base = layers * tokens

        def store(layer, row, value):
            inverse_ref[layer, row : row + 1, :] = value

        inverse_factors([total[:, base + l * rank : base + (l + 1) * rank] for l in range(layers)], store)
        for l in range(layers):
            proj[l] = jnp.dot(
                inverse_ref[l],
                total[:, l * tokens : (l + 1) * tokens],
                precision=lax.Precision.HIGHEST,
                preferred_element_type=F32,
            ).astype(BF16)

    left = proj[pl.program_id(0)]
    wide = 2 * LANES
    for tile in range(grad_ref.shape[2] // wide):
        got = jnp.dot(left, grad_ref[0, :, tile * wide : (tile + 1) * wide], preferred_element_type=F32)
        got = (got * scale).astype(BF16)
        out_ref[0, 2 * tile] = got[:, :LANES]
        out_ref[0, 2 * tile + 1] = got[:, LANES:]


def right_of(mine, theirs, grad, scale):
    layers, tokens, hidden = grad.shape
    rank, width = mine.shape
    steps = 4
    block = hidden // steps
    tiles = block // LANES

    def body(*refs):
        right_body(scale, *refs)

    return pl.pallas_call(
        body,
        grid=(layers, steps),
        in_specs=[
            pl.BlockSpec((rank, width), lambda l, k: (0, 0)),
            pl.BlockSpec((rank, width), lambda l, k: (0, 0)),
            pl.BlockSpec((1, tokens, block), lambda l, k: (l, 0, k)),
        ],
        out_specs=[
            pl.BlockSpec((layers, rank, rank), lambda l, k: (0, 0, 0)),
            pl.BlockSpec((1, tiles, rank, LANES), lambda l, k: (l, k, 0, 0)),
        ],
        out_shape=[
            jax.ShapeDtypeStruct((layers, rank, rank), F32),
            jax.ShapeDtypeStruct((layers, hidden // LANES, rank, LANES), BF16),
        ],
        scratch_shapes=[pltpu.VMEM((layers, rank, tokens), BF16)],
        compiler_params=params(24),
        name="right",
    )(mine, theirs, grad)


def hat_body(inverse_ref, p_ref, out_ref):
    rank = inverse_ref.shape[1]
    stacked = jnp.concatenate(split3(inverse_ref[0]), axis=0)
    for tile in range(p_ref.shape[1]):
        got = jnp.dot(stacked, p_ref[0, tile], preferred_element_type=F32)
        got = (got[2 * rank :] + got[rank : 2 * rank]) + got[:rank]
        out_ref[0, :, tile * LANES : (tile + 1) * LANES] = got


def hat_of(inverse, p_blocks):
    layers, tiles, rank, _ = p_blocks.shape
    return pl.pallas_call(
        hat_body,
        grid=(layers,),
        in_specs=[
            pl.BlockSpec((1, rank, rank), lambda l: (l, 0, 0)),
            pl.BlockSpec((1, tiles, rank, LANES), lambda l: (l, 0, 0, 0)),
        ],
        out_specs=pl.BlockSpec((1, rank, tiles * LANES), lambda l: (l, 0, 0)),
        out_shape=jax.ShapeDtypeStruct((layers, rank, tiles * LANES), F32),
        compiler_params=params(24),
        name="hat",
    )(inverse, p_blocks)


def widen_body(in_ref, out_ref):
    for tile in range(in_ref.shape[1]):
        out_ref[0, :, tile * LANES : (tile + 1) * LANES] = in_ref[0, tile].astype(F32)


def widen(blocks):
    layers, tiles, rank, _ = blocks.shape
    steps = 2
    return pl.pallas_call(
        widen_body,
        grid=(layers, steps),
        in_specs=[pl.BlockSpec((1, tiles // steps, rank, LANES), lambda l, k: (l, k, 0, 0))],
        out_specs=pl.BlockSpec((1, rank, tiles // steps * LANES), lambda l, k: (l, 0, k)),
        out_shape=jax.ShapeDtypeStruct((layers, rank, tiles * LANES), F32),
        compiler_params=params(24),
        name="widen",
    )(blocks)


def exchange(value, axes):
    return lax.all_to_all(value, axes, 0, 0, tiled=True)


def add_up(value):
    return jnp.sum(value.astype(F32), axis=0).astype(BF16)


def copies(value, count):
    return jnp.broadcast_to(value[None], (count, *value.shape))


def sum_over_chips(blocks):
    near, far = lax.axis_size(NEAR), lax.axis_size(FAR)
    shape = blocks.shape
    chunks = blocks.reshape(near, -1, LANES)
    chunk = add_up(exchange(chunks, NEAR))
    chunk = add_up(exchange(copies(chunk, far), FAR))
    return exchange(copies(chunk, near), NEAR).reshape(shape)


def on_device(x_saved, grad_pre, q_prev):
    half = x_saved.shape[2] // 2
    token_count = grad_pre.shape[1] * lax.axis_size(CHIPS)
    scale = float(token_count) ** (-0.5)
    core = lax.axis_index(CORE)
    core_array = core.reshape(1)
    x_in = swap(lax.dynamic_slice_in_dim(x_saved, (1 - core) * half, half, axis=2))
    mine = partial_of(grad_pre, jnp.swapaxes(q_prev, 1, 2))
    theirs = swap(mine)
    p_blocks = sum_over_chips(left_of(core_array, x_saved, x_in, mine, theirs))
    inner = inner_of(core_array, x_saved, x_in, p_blocks)
    inverse, q_blocks = right_of(inner, swap(inner), grad_pre, scale)
    p_hat = hat_of(inverse, p_blocks)
    q_new = widen(sum_over_chips(q_blocks))
    return jnp.swapaxes(p_hat, 1, 2), jnp.swapaxes(q_new, 1, 2)


def solution(mesh):
    dims = (4, 2, 4, 4, 2)
    fine = Mesh(mesh.devices.reshape(dims), (*CHIPS, CORE))
    placed = (
        P(None, (*CHIPS, CORE), None),
        P(None, CHIPS, CORE),
        P(None, CORE, None),
    )
    return jax.shard_map(
        on_device,
        mesh=fine,
        in_specs=placed,
        out_specs=(P(None, CORE, None), P(None, CORE, None)),
        check_vma=False,
    )
```

time: 1080 us -> 147 us (0.14)
  blocking collectives: 706 us -> 93 us
  waiting for transfers between devices: 295 us -> 16.9 us
  other arithmetic: 30.9 us -> 0.37 us
  matrix products: 29.4 us -> 0 us
  Pallas kernels: 0 us -> 19.1 us
  between operations: 13.9 us -> 0.74 us
    psum x2 -> x0, blocking collectives: 701 us -> none  [the longest x1 697 us: compress(): p_rows = lax.psum(p_rows, 'dp')]
    psum x1 -> x0, waiting for transfers between devices: 231 us -> none  [compress(): q_new = lax.psum(q_part * norm_scale, 'dp')]
    all_to_all x0 -> x5, blocking collectives: none -> 93 us  [exchange(): return lax.all_to_all(value, axes, 0, 0, tiled=True)]
    all_gather x2 -> x0, waiting for transfers between devices: 34.2 us -> none  [compress(): full_x = lax.all_gather(x_saved, 'tensor', axis=1, tiled=True)]
    reduce_scatter x2 -> x0, waiting for transfers between devices: 29.4 us -> none  [compress(): lax.psum_scatter(p_part.astype(jnp.bfloat16), 'tensor', scatter_dimension...]
    dot_general x6 -> x0, matrix products: 26.5 us -> none  [the longest x2 12.4 us: compress(): jnp.einsum('ltd,ltr->ldr', full_x, partial_value, preferred_element_type=...]
    another operation x11 -> x0, other arithmetic: 26 us -> none  [the longest x6 13 us: normalize(): lower_factor = jnp.linalg.cholesky(gram_matrix)]
    pallas_call x0 -> x6, Pallas kernels: none -> 19.1 us  [the longest x1 8.11 us: right_of(): pl.pallas_call(body, grid=(layers, steps), in_specs=[pl.BlockSpec((rank,...]
  transfers between devices with their start and end apart: 5 -> 4, of which waited for: 5 -> 3; matrix products, arithmetic and copies ran while one was open for 1% -> 0% of each run, Pallas kernels for 0% -> 4%
where the time goes in v1:
time: 147 us; the launch traced here: 146 us
  blocking collectives  93 us (63%)
  Pallas kernels  19.1 us (13%)
  waiting for transfers between devices  16.9 us (11%)
  local copies, waits for them, and re-layouts  10.6 us (7%)
  starting transfers between devices  5.62 us (4%)
    all_to_all x5, blocking collectives, exchange(): return lax.all_to_all(value, axes, 0, 0, tiled=True)  93 us
    all_to_all x1, waiting for transfers between devices, exchange(): return lax.all_to_all(value, axes, 0, 0, tiled=True)  14.4 us
    pallas_call x1, Pallas kernels, right_of(): pl.pallas_call(body, grid=(layers, steps), in_specs=[pl.BlockSpec((rank,...  8.11 us
    unnamed x10, local copies, waits for them, and re-layouts  7.42 us
    all_to_all x1, starting transfers between devices, exchange(): return lax.all_to_all(value, axes, 0, 0, tiled=True)  5.26 us
    pallas_call x1, Pallas kernels, partial_of(): pl.pallas_call(partial_body, grid=(layers, steps), in_specs=[pl.BlockSpec...  3.43 us
  transfers between devices with their start and end apart: 4, of which 3 were waited for; matrix products, arithmetic and copies ran while one was open for 0% of the time, Pallas kernels for 4%

profile of v1, /device:TPU:8, one launch (start us, length us, event | category | flops | bytes accessed | tf_op | source)
XLA Modules:
  0.0 146.4 jit_solution(5670439860981292751)
XLA Ops:
  0.6 0.0 copy-start.4
  0.6 1.8 %constant_dynamic-slice_fusion = bf16[2,128,3584]{2,1,0:T(8,128)(2,1)S(1)} fusion(bf16[2,128,7168]{2,1,0:T(8,128)(2,1)} %own_ref.3, s32[]{:T(128)S(6)} %select_n.3), kind=kLoop, calls=%fused_computation | loop fusion | bytes 3670020 | tf_op jit(solution)/shard_map/dynamic_slice | solution.py:332
  2.4 0.1 collective-permute-start
  2.5 0.4 copy-done.4
  2.9 0.0 copy-start.2
  2.9 2.5 %copy-done.2 = bf16[2,256,5120]{2,1,0:T(8,128)(2,1)S(1)} copy-done((bf16[2,256,5120]{2,1,0:T(8,128)(2,1)S(1)}, bf16[2,256,5120]{2,1,0:T(8,128)(2,1)}, u32[]{:S(2)}) %copy-start.2) | copy-done | bytes 5242904
  5.4 0.0 copy-start
  5.4 3.4 %partial.1.mine_ref = bf16[2,64,256]{2,1,0:T(8,128)(2,1)S(1)} custom-call(bf16[2,256,5120]{2,1,0:T(8,128)(2,1)S(1)} %copy-done.2, f32[2,64,5120]{2,1,0:T(8,128)S(1)} %bitcast.12), custom_call_target="tpu_custom_call" | custom-call | tf_op jit(solution)/shard_map/partial/pallas_call | solution.py:47
  8.9 0.2 collective-permute-start.1
  9.0 1.2 collective-permute-done.1.theirs_ref
  10.2 0.0 collective-permute-done.in_ref
  10.2 0.0 copy-done
  10.2 1.6 %left.1 = bf16[2,28,64,128]{3,2,1,0:T(8,128)(2,1)S(1)} custom-call(s32[1]{0:T(128)} %bitcast.core_ref, bf16[2,128,7168]{2,1,0:T(8,128)(2,1)S(1)} %copy-done, bf16[2,128,3584]{2,1,0:T(8,128)(2,1)S(1)} %collective-permute-done.in_ref, bf16[2,64,256]{2,1,0:T(8,128)(2,1)S(1)} %partial.1.mine_ref, bf16[2,64,256]{2,1,0:T(8,128)(2,1)S(1)} %collective-permute-done.1.theirs_ref), custom_call_target="tpu_custom_call" | custom-call | tf_op jit(solution)/shard_map/left/pallas_call | solution.py:92
  11.8 23.6 %all_to_all.30 = bf16[32,112,128]{2,1,0:T(8,128)(2,1)S(1)} all-to-all(bf16[32,112,128]{2,1,0:T(8,128)(2,1)S(1)} %bitcast.11), channel_id=1, replica_groups=mesh['zh'=4,'zl'=2,'y'=4,'x'=4,'core'=2] {'zl','x','y'}, dimensions={0} | all-to-all | bytes 1835008 | tf_op jit(solution)/shard_map/all_to_all | solution.py:306
  35.4 0.1 reduce_sum.48
  35.5 15.7 %all_to_all.31 = bf16[4,112,128]{2,1,0:T(8,128)(2,1)S(1)} all-to-all(bf16[4,112,128]{2,1,0:T(8,128)(2,1)S(1)} %broadcast_in_dim.8), channel_id=1, replica_groups=mesh['zh'=4,'zl'=2,'y'=4,'x'=4,'core'=2] {'zh'}, dimensions={0} | all-to-all | bytes 229376 | tf_op jit(solution)/shard_map/all_to_all | solution.py:306
  51.2 0.1 broadcast_in_dim.9
  51.3 17.8 %all_to_all.32 = bf16[32,112,128]{2,1,0:T(8,128)(2,1)S(1)} all-to-all(bf16[32,112,128]{2,1,0:T(8,128)(2,1)S(1)} %broadcast_in_dim.9), channel_id=1, replica_groups=mesh['zh'=4,'zl'=2,'y'=4,'x'=4,'core'=2] {'zl','x','y'}, dimensions={0} | all-to-all | bytes 1835008 | tf_op jit(solution)/shard_map/all_to_all | solution.py:306
  69.1 2.0 %copy-done.1 = bf16[2,128,7168]{2,1,0:T(8,128)(2,1)S(1)} copy-done((bf16[2,128,7168]{2,1,0:T(8,128)(2,1)S(1)}, bf16[2,128,7168]{2,1,0:T(8,128)(2,1)}, u32[]{:S(2)}) %copy-start.1) | copy-done | bytes 3670040
  71.2 2.0 %inner.1.refs_0_ = f32[64,640]{1,0:T(8,128)S(1)} custom-call(s32[1]{0:T(128)} %bitcast.core_ref, bf16[2,128,7168]{2,1,0:T(8,128)(2,1)S(1)} %copy-done.1, bf16[2,128,3584]{2,1,0:T(8,128)(2,1)S(1)} %collective-permute-done.in_ref, bf16[2,28,64,128]{3,2,1,0:T(8,128)(2,1)S(1)} %bitcast.8), custom_call_target="tpu_custom_call" | custom-call | tf_op jit(solution)/shard_map/inner/pallas_call | solution.py:140
  73.2 0.1 collective-permute-start.2
  73.3 1.4 collective-permute-done.2.refs_1_
  74.7 2.5 %copy-done.3 = bf16[2,256,5120]{2,1,0:T(8,128)(2,1)S(1)} copy-done((bf16[2,256,5120]{2,1,0:T(8,128)(2,1)S(1)}, bf16[2,256,5120]{2,1,0:T(8,128)(2,1)}, u32[]{:S(2)}) %copy-start.3) | copy-done | bytes 5242904
  77.1 8.1 %right.1 = (f32[2,64,64]{2,1,0:T(8,128)S(1)}, bf16[2,40,64,128]{3,2,1,0:T(8,128)(2,1)S(1)}) custom-call(f32[64,640]{1,0:T(8,128)S(1)} %inner.1.refs_0_, f32[64,640]{1,0:T(8,128)S(1)} %collective-permute-done.2.refs_1_, bf16[2,256,5120]{2,1,0:T(8,128)(2,1)S(1)} %copy-done.3), custom_call_target="tpu_custom_call" | custom-call | tf_op jit(solution)/shard_map/right/pallas_call | solution.py:239
  85.3 24.4 %all_to_all.33 = bf16[32,160,128]{2,1,0:T(8,128)(2,1)S(1)} all-to-all(bf16[32,160,128]{2,1,0:T(8,128)(2,1)S(1)} %bitcast.13), channel_id=1, replica_groups=mesh['zh'=4,'zl'=2,'y'=4,'x'=4,'core'=2] {'zl','x','y'}, dimensions={0} | all-to-all | bytes 2621440 | tf_op jit(solution)/shard_map/all_to_all | solution.py:306
  109.7 0.2 reduce_sum.50
  109.9 11.6 %all_to_all.34 = bf16[4,160,128]{2,1,0:T(8,128)(2,1)S(1)} all-to-all(bf16[4,160,128]{2,1,0:T(8,128)(2,1)S(1)} %broadcast_in_dim.10), channel_id=1, replica_groups=mesh['zh'=4,'zl'=2,'y'=4,'x'=4,'core'=2] {'zh'}, dimensions={0} | all-to-all | bytes 327680 | tf_op jit(solution)/shard_map/all_to_all | solution.py:306
  121.5 1.2 broadcast_in_dim.11
  122.7 5.3 %all-to-all-start.5 = ((bf16[32,160,128]{2,1,0:T(8,128)(2,1)}), bf16[32,160,128]{2,1,0:T(8,128)(2,1)S(1)}, u32[]{:S(2)}, u32[]{:S(2)}) async-start(bf16[32,160,128]{2,1,0:T(8,128)(2,1)} %broadcast_in_dim.11), calls=%async_computation.5 | async-start | bytes 2621440 | tf_op jit(solution)/shard_map/all_to_all | solution.py:306
  128.0 2.0 %hat.1 = f32[2,64,3584]{2,1,0:T(8,128)} custom-call(f32[2,64,64]{2,1,0:T(8,128)S(1)} %get-tuple-element.4.inverse_ref, bf16[2,28,64,128]{3,2,1,0:T(8,128)(2,1)S(1)} %bitcast.9), custom_call_target="tpu_custom_call" | custom-call | tf_op jit(solution)/shard_map/hat/pallas_call | solution.py:272
  130.0 14.4 %all-to-all-done.5 = bf16[32,160,128]{2,1,0:T(8,128)(2,1)S(1)} async-done(((bf16[32,160,128]{2,1,0:T(8,128)(2,1)}), bf16[32,160,128]{2,1,0:T(8,128)(2,1)S(1)}, u32[]{:S(2)}, u32[]{:S(2)}) %all-to-all-start.5) | async-done | bytes 1310752 | tf_op jit(solution)/shard_map/all_to_all | solution.py:306
  144.4 2.0 %widen.1 = f32[2,64,5120]{2,1,0:T(8,128)} custom-call(bf16[2,40,64,128]{3,2,1,0:T(8,128)(2,1)S(1)} %bitcast.10), custom_call_target="tpu_custom_call" | custom-call | tf_op jit(solution)/shard_map/widen/pallas_call | solution.py:294
  (6 shorter events, 0.1 us)
Async XLA Ops:
  0.6 2.3 %copy-start.4 = (f32[2,5120,64]{1,2,0:T(8,128)S(1)}, f32[2,5120,64]{1,2,0:T(8,128)}, u32[]{:S(2)}) copy-start(f32[2,5120,64]{1,2,0:T(8,128)} %param.5) | copy-start | bytes 7864324
  2.4 7.8 %collective-permute-start = (bf16[2,128,3584]{2,1,0:T(8,128)(2,1)S(1)}, bf16[2,128,3584]{2,1,0:T(8,128)(2,1)S(1)}, u32[]{:S(2)}, u32[]{:S(2)}) collective-permute-start(bf16[2,128,3584]{2,1,0:T(8,128)(2,1)S(1)} %constant_dynamic-slice_fusion), channel_id=1, source_target_pairs={{0,1},{1,0},{2,3},{3,2},{4,5},{5,4},{6,7},{7,6},{8,9},{9,8},{10,11... | collective-permute-start | bytes 5505032 | tf_op jit(solution)/shard_map/ppermute | solution.py:23
  2.9 2.5 %copy-start.2 = (bf16[2,256,5120]{2,1,0:T(8,128)(2,1)S(1)}, bf16[2,256,5120]{2,1,0:T(8,128)(2,1)}, u32[]{:S(2)}) copy-start(bf16[2,256,5120]{2,1,0:T(8,128)(2,1)} %refs_2_.1) | copy-start | bytes 15728644
  5.4 4.8 %copy-start = (bf16[2,128,7168]{2,1,0:T(8,128)(2,1)S(1)}, bf16[2,128,7168]{2,1,0:T(8,128)(2,1)}, u32[]{:S(2)}) copy-start(bf16[2,128,7168]{2,1,0:T(8,128)(2,1)} %own_ref.3) | copy-start | bytes 11010052
  8.9 1.3 collective-permute-start.1
  69.1 2.0 %copy-start.1 = (bf16[2,128,7168]{2,1,0:T(8,128)(2,1)S(1)}, bf16[2,128,7168]{2,1,0:T(8,128)(2,1)}, u32[]{:S(2)}) copy-start(bf16[2,128,7168]{2,1,0:T(8,128)(2,1)} %own_ref.3) | copy-start | bytes 11010052
  73.2 1.5 %collective-permute-start.2 = (f32[64,640]{1,0:T(8,128)S(1)}, f32[64,640]{1,0:T(8,128)S(1)}, u32[]{:S(2)}, u32[]{:S(2)}) collective-permute-start(f32[64,640]{1,0:T(8,128)S(1)} %inner.1.refs_0_), channel_id=1, source_target_pairs={{0,1},{1,0},{2,3},{3,2},{4,5},{5,4},{6,7},{7,6},{8,9},{9,8},{10,11... | collective-permute-start | bytes 491528 | tf_op jit(solution)/shard_map/ppermute | solution.py:23
  74.6 2.5 %copy-start.3 = (bf16[2,256,5120]{2,1,0:T(8,128)(2,1)S(1)}, bf16[2,256,5120]{2,1,0:T(8,128)(2,1)}, u32[]{:S(2)}) copy-start(bf16[2,256,5120]{2,1,0:T(8,128)(2,1)} %refs_2_.1) | copy-start | bytes 15728644
  122.7 21.7 %all-to-all-start.5 = ((bf16[32,160,128]{2,1,0:T(8,128)(2,1)}), bf16[32,160,128]{2,1,0:T(8,128)(2,1)S(1)}, u32[]{:S(2)}, u32[]{:S(2)}) async-start(bf16[32,160,128]{2,1,0:T(8,128)(2,1)} %broadcast_in_dim.11), calls=%async_computation.5 | async-start | bytes 2621440 | tf_op jit(solution)/shard_map/all_to_all | solution.py:306

commit v2 on v0

v2 whole, which is shorter than its diff:
```python
import jax
import jax.numpy as jnp
from jax import lax
from jax.experimental import pallas as pl
from jax.experimental.pallas import tpu as pltpu
from jax.sharding import Mesh
from jax.sharding import PartitionSpec as P

LANES = 128
P_NEAR, Q_NEAR = ("zl", "y", "x"), ("x", "y", "zl")
FAR = ("zh",)
CHIPS = ("zh", "zl", "y", "x")
CORE = "core"
F32, BF16 = jnp.float32, jnp.bfloat16
TRANSPOSED = (((1,), (1,)), ((), ()))
FAR_MEMORY = pl.BlockSpec(memory_space=pltpu.HBM)
WHOLE = pl.BlockSpec(memory_space=pltpu.VMEM)
SCALAR = pl.BlockSpec(memory_space=pltpu.SMEM)


def params(mib):
    return pltpu.CompilerParams(vmem_limit_bytes=mib << 20)


def stay(value):
    return pltpu.with_memory_space_constraint(value, pltpu.HBM)


def near(value):
    return pltpu.with_memory_space_constraint(value, pltpu.VMEM)


def swap(value):
    return lax.ppermute(value, CORE, [(0, 1), (1, 0)])


def half_body(core_ref, x_ref, out_ref, sem):
    half = out_ref.shape[2]
    start = pl.multiple_of((1 - core_ref[0]) * half, LANES)
    move = pltpu.make_async_copy(x_ref.at[:, :, pl.ds(start, half)], out_ref, sem)
    move.start()
    move.wait()


def half_of(core, x):
    layers, tokens, width = x.shape
    return pl.pallas_call(
        half_body,
        in_specs=[SCALAR, FAR_MEMORY],
        out_specs=WHOLE,
        out_shape=pltpu.VMEM((layers, tokens, width // 2), BF16),
        scratch_shapes=[pltpu.SemaphoreType.DMA],
        compiler_params=params(2),
        name="half",
    )(core, stay(x))


def partial_body(core_ref, grad_ref, q_ref, x_ref, out_ref, x_held, grad_held, q_held, sems, x_sem):
    layers, _, hidden = grad_ref.shape
    half = x_held.shape[2]
    steps = sems.shape[2]
    block = hidden // steps
    moves = {}
    for l in range(layers):
        for k in range(steps):
            at = pl.ds(k * block, block)
            for index, (here, held) in enumerate(((q_ref, q_held), (grad_ref, grad_held))):
                moves[l, k, index] = pltpu.make_async_copy(
                    here.at[l, :, at], held.at[l, :, at], sems.at[index, l, k]
                )
                moves[l, k, index].start()
    start = pl.multiple_of(core_ref[0] * half, LANES)
    x_move = pltpu.make_async_copy(x_ref.at[:, :, pl.ds(start, half)], x_held, x_sem)
    x_move.start()
    for l in range(layers):
        total = None
        for k in range(steps):
            moves[l, k, 0].wait()
            moves[l, k, 1].wait()
            at = slice(k * block, (k + 1) * block)
            got = lax.dot_general(
                grad_held[l, :, at], q_held[l, :, at].astype(BF16), TRANSPOSED, preferred_element_type=F32
            )
            total = got if total is None else total + got
        out_ref[l] = total.T.astype(BF16)
    x_move.wait()


def partial_of(core, grad, q_rows, x):
    layers, tokens, hidden = grad.shape
    rank = q_rows.shape[1]
    _, own, width = x.shape
    steps = 4
    return pl.pallas_call(
        partial_body,
        in_specs=[SCALAR, FAR_MEMORY, FAR_MEMORY, FAR_MEMORY],
        out_specs=[WHOLE, WHOLE],
        out_shape=[
            pltpu.VMEM((layers, rank, tokens), BF16),
            pltpu.VMEM((layers, own, width // 2), BF16),
        ],
        scratch_shapes=[
            pltpu.VMEM((layers, tokens, hidden), BF16),
            pltpu.VMEM((layers, rank, hidden), F32),
            pltpu.SemaphoreType.DMA((2, layers, steps)),
            pltpu.SemaphoreType.DMA,
        ],
        compiler_params=params(12),
        name="partial",
    )(core, stay(grad), stay(q_rows), stay(x))


def fetch_body(grad_ref, out_ref, sems):
    moves = [pltpu.make_async_copy(grad_ref.at[l], out_ref.at[l], sems.at[l]) for l in range(out_ref.shape[0])]
    for move in moves:
        move.start()
    for move in moves:
        move.wait()


def fetch(grad):
    return pl.pallas_call(
        fetch_body,
        in_specs=[FAR_MEMORY],
        out_specs=WHOLE,
        out_shape=pltpu.VMEM(grad.shape, BF16),
        scratch_shapes=[pltpu.SemaphoreType.DMA((grad.shape[0],))],
        cost_estimate=pl.CostEstimate(flops=0, bytes_accessed=4 * grad.size, transcendentals=0),
        compiler_params=params(4),
        name="fetch",
    )(stay(grad))


def own_first(core, value):
    mid = value.shape[1] // 2
    low, high = value[:, :mid], value[:, mid:]
    return jnp.concatenate(
        [jnp.where(core == 0, low, high), jnp.where(core == 0, high, low)], axis=1
    )


def left_body(core_ref, own_ref, in_ref, mine_ref, theirs_ref, out_ref):
    core = core_ref[0]
    layers, rank = mine_ref.shape[:2]
    wide = 2 * LANES
    for l in range(layers):
        both = jnp.concatenate(
            [own_first(core, mine_ref[l].astype(F32)), own_first(core, theirs_ref[l].astype(F32))], axis=0
        ).astype(BF16)
        for tile in range(own_ref.shape[2] // wide):
            at = slice(tile * wide, (tile + 1) * wide)
            rows = jnp.concatenate([own_ref[l, :, at], in_ref[l, :, at]], axis=0)
            got = jnp.dot(both, rows, preferred_element_type=F32)
            got = (got[:rank] + got[rank:]).astype(BF16)
            out_ref[l, 2 * tile] = got[:, :LANES]
            out_ref[l, 2 * tile + 1] = got[:, LANES:]


def left_of(core, x_own, x_in, mine, theirs):
    layers, _, half = x_in.shape
    rank = mine.shape[1]
    return pl.pallas_call(
        left_body,
        in_specs=[SCALAR, WHOLE, WHOLE, WHOLE, WHOLE],
        out_specs=WHOLE,
        out_shape=pltpu.VMEM((layers, half // LANES, rank, LANES), BF16),
        compiler_params=params(6),
        name="left",
    )(core, near(x_own), near(x_in), near(mine), near(theirs))


def inner_body(core_ref, own_ref, in_ref, p_ref, out_ref):
    core = core_ref[0]
    layers, tiles, rank, _ = p_ref.shape
    tokens = 2 * own_ref.shape[1]
    base = layers * tokens
    for l in range(layers):
        rows = jnp.concatenate([p_ref[l, tile] for tile in range(tiles)], axis=1)
        seen = jnp.concatenate([own_ref[l], in_ref[l]], axis=0)
        got = lax.dot_general(rows, seen, TRANSPOSED, preferred_element_type=F32)
        out_ref[:, l * tokens : (l + 1) * tokens] = own_first(core, got)
        got = lax.dot_general(rows, rows, TRANSPOSED, preferred_element_type=F32)
        out_ref[:, base + l * rank : base + (l + 1) * rank] = got


def inner_of(core, x_own, x_in, p_blocks):
    layers, tokens, _ = x_in.shape
    rank = p_blocks.shape[2]
    width = layers * (2 * tokens + rank)
    return pl.pallas_call(
        inner_body,
        in_specs=[SCALAR, WHOLE, WHOLE, WHOLE],
        out_specs=WHOLE,
        out_shape=pltpu.VMEM((rank, width), F32),
        compiler_params=params(8),
        name="inner",
    )(core, near(x_own), near(x_in), near(p_blocks))


def inverse_factors(grams, store):
    rank = grams[0].shape[0]
    height = 8
    blocks = rank // height
    shape = (height, 2 * rank)
    line = lax.broadcasted_iota(jnp.int32, (height, rank), 0)
    column = lax.broadcasted_iota(jnp.int32, (height, rank), 1)
    state = [
        [
            jnp.concatenate(
                [
                    gram[b * height : (b + 1) * height],
                    jnp.where(column == line + b * height, 1.0, 0.0).astype(F32),
                ],
                axis=1,
            )
            for b in range(blocks)
        ]
        for gram in grams
    ]

    def full(value):
        return jnp.broadcast_to(value, shape)

    for at in range(blocks):
        first = at * height
        for index, rows in enumerate(state):
            pivots = [full(rows[at][k : k + 1]) for k in range(height)]
            corners = {
                (k, m): full(pivots[k][:, first + m : first + m + 1]) for k in range(height) for m in range(k, height)
            }
            columns = {
                b: [full(rows[b][:, first + k : first + k + 1]) for k in range(height)]
                for b in range(at + 1, blocks)
            }
            scaled, roots, factors = [], [], {}
            for k in range(height):
                corner, row = corners[k, k], pivots[k]
                for q in range(k):
                    corner = corner - factors[q, k] * factors[q, k]
                roots.append(lax.rsqrt(corner))
                for q in range(k):
                    row = row - factors[q, k] * scaled[q]
                scaled.append(row * roots[k])
                for m in range(k + 1, height):
                    value = corners[k, m]
                    for q in range(k):
                        value = value - factors[q, k] * factors[q, m]
                    factors[k, m] = value * roots[k]
            for k in range(height):
                store(index, first + k, scaled[k][:1, rank:])
            for b in range(at + 1, blocks):
                lower = []
                for k in range(height):
                    value = columns[b][k]
                    for q in range(k):
                        value = value - lower[q] * factors[q, k]
                    lower.append(value * roots[k])
                for k in range(height):
                    rows[b] = rows[b] - lower[k] * scaled[k]


def split3(value):
    high = value.astype(BF16)
    rest = value - high.astype(F32)
    mid = rest.astype(BF16)
    return high, mid, (rest - mid.astype(F32)).astype(BF16)


def right_body(scale, mine_ref, theirs_ref, grad_ref, inverse_ref, out_ref):
    layers, tokens, hidden = grad_ref.shape
    rank = mine_ref.shape[0]
    total = mine_ref[...] + theirs_ref[...]
    base = layers * tokens

    def store(layer, row, value):
        inverse_ref[layer, row : row + 1, :] = value

    inverse_factors([total[:, base + l * rank : base + (l + 1) * rank] for l in range(layers)], store)
    wide = 2 * LANES
    for l in range(layers):
        left = jnp.dot(
            inverse_ref[l],
            total[:, l * tokens : (l + 1) * tokens],
            precision=lax.Precision.HIGHEST,
            preferred_element_type=F32,
        ).astype(BF16)
        for tile in range(hidden // wide):
            got = jnp.dot(left, grad_ref[l, :, tile * wide : (tile + 1) * wide], preferred_element_type=F32)
            got = (got * scale).astype(BF16)
            out_ref[l, 2 * tile] = got[:, :LANES]
            out_ref[l, 2 * tile + 1] = got[:, LANES:]


def right_of(mine, theirs, grad, scale):
    layers, _, hidden = grad.shape
    rank, _ = mine.shape

    def body(*refs):
        right_body(scale, *refs)

    return pl.pallas_call(
        body,
        in_specs=[WHOLE, WHOLE, WHOLE],
        out_specs=[WHOLE, WHOLE],
        out_shape=[
            pltpu.VMEM((layers, rank, rank), F32),
            pltpu.VMEM((layers, hidden // LANES, rank, LANES), BF16),
        ],
        compiler_params=params(8),
        name="right",
    )(near(mine), near(theirs), near(grad))


def finish_body(inverse_ref, p_ref, q_ref, hat_ref, new_ref):
    rank = inverse_ref.shape[1]
    wide = 2 * LANES
    for tile in range(q_ref.shape[1]):
        new_ref[0, :, tile * LANES : (tile + 1) * LANES] = q_ref[0, tile].astype(F32)
    stacked = jnp.concatenate(split3(inverse_ref[0]), axis=0)
    for tile in range(p_ref.shape[1] // 2):
        rows = jnp.concatenate([p_ref[0, 2 * tile], p_ref[0, 2 * tile + 1]], axis=1)
        got = jnp.dot(stacked, rows, preferred_element_type=F32)
        got = (got[2 * rank :] + got[rank : 2 * rank]) + got[:rank]
        hat_ref[0, :, tile * wide : (tile + 1) * wide] = got


def finish(inverse, p_blocks, q_blocks):
    layers, p_tiles, rank, _ = p_blocks.shape
    q_tiles = q_blocks.shape[1]
    steps = 2
    return pl.pallas_call(
        finish_body,
        grid=(layers, steps),
        in_specs=[
            pl.BlockSpec((1, rank, rank), lambda l, k: (l, 0, 0)),
            pl.BlockSpec((1, p_tiles // steps, rank, LANES), lambda l, k: (l, k, 0, 0)),
            pl.BlockSpec((1, q_tiles // steps, rank, LANES), lambda l, k: (l, k, 0, 0)),
        ],
        out_specs=[
            pl.BlockSpec((1, rank, p_tiles // steps * LANES), lambda l, k: (l, 0, k)),
            pl.BlockSpec((1, rank, q_tiles // steps * LANES), lambda l, k: (l, 0, k)),
        ],
        out_shape=[
            jax.ShapeDtypeStruct((layers, rank, p_tiles * LANES), F32),
            jax.ShapeDtypeStruct((layers, rank, q_tiles * LANES), F32),
        ],
        compiler_params=params(12),
        name="finish",
    )(inverse, p_blocks, q_blocks)


def exchange(value, axes):
    return lax.all_to_all(value, axes, 0, 0, tiled=True)


def add_up(value):
    return jnp.sum(value.astype(F32), axis=0).astype(BF16)


def copies(value, count):
    return jnp.broadcast_to(value[None], (count, *value.shape))


def sum_over_chips(blocks, group):
    inside, outside = lax.axis_size(group), lax.axis_size(FAR)
    shape = blocks.shape
    chunks = blocks.reshape(inside, -1, LANES)
    chunk = add_up(exchange(chunks, group))
    chunk = add_up(exchange(copies(chunk, outside), FAR))
    return exchange(copies(chunk, inside), group).reshape(shape)


def on_device(x_saved, grad_pre, q_prev):
    token_count = grad_pre.shape[1] * lax.axis_size(CHIPS)
    scale = float(token_count) ** (-0.5)
    core = lax.axis_index(CORE)
    core_array = core.reshape(1)
    x_in = swap(half_of(core_array, x_saved))
    mine, x_own = partial_of(core_array, grad_pre, jnp.swapaxes(q_prev, 1, 2), x_saved)
    theirs = swap(mine)
    p_blocks = sum_over_chips(left_of(core_array, x_own, x_in, mine, theirs), P_NEAR)
    inner = inner_of(core_array, x_own, x_in, p_blocks)
    grad, tied = lax.optimization_barrier((grad_pre, inner))
    inverse, q_blocks = right_of(tied, swap(tied), fetch(grad), scale)
    p_hat, q_new = finish(inverse, p_blocks, sum_over_chips(q_blocks, Q_NEAR))
    return jnp.swapaxes(p_hat, 1, 2), jnp.swapaxes(q_new, 1, 2)


def solution(mesh):
    dims = (4, 2, 4, 4, 2)
    fine = Mesh(mesh.devices.reshape(dims), (*CHIPS, CORE))
    placed = (
        P(None, (*CHIPS, CORE), None),
        P(None, CHIPS, CORE),
        P(None, CORE, None),
    )
    return jax.shard_map(
        on_device,
        mesh=fine,
        in_specs=placed,
        out_specs=(P(None, CORE, None), P(None, CORE, None)),
        check_vma=False,
    )
```

time: 1080 us -> 139 us (0.13)
  blocking collectives: 706 us -> 117 us
  waiting for transfers between devices: 295 us -> 0.91 us
  other arithmetic: 30.9 us -> 0.37 us
  matrix products: 29.4 us -> 0 us
  Pallas kernels: 0 us -> 18.1 us
  between operations: 13.9 us -> 0.76 us
    psum x2 -> x0, blocking collectives: 701 us -> none  [the longest x1 697 us: compress(): p_rows = lax.psum(p_rows, 'dp')]
    psum x1 -> x0, waiting for transfers between devices: 231 us -> none  [compress(): q_new = lax.psum(q_part * norm_scale, 'dp')]
    all_to_all x0 -> x6, blocking collectives: none -> 117 us  [exchange(): return lax.all_to_all(value, axes, 0, 0, tiled=True)]
    all_gather x2 -> x0, waiting for transfers between devices: 34.2 us -> none  [compress(): full_x = lax.all_gather(x_saved, 'tensor', axis=1, tiled=True)]
    reduce_scatter x2 -> x0, waiting for transfers between devices: 29.4 us -> none  [compress(): lax.psum_scatter(p_part.astype(jnp.bfloat16), 'tensor', scatter_dimension...]
    dot_general x6 -> x0, matrix products: 26.5 us -> none  [the longest x2 12.4 us: compress(): jnp.einsum('ltd,ltr->ldr', full_x, partial_value, preferred_element_type=...]
    another operation x11 -> x0, other arithmetic: 26 us -> none  [the longest x6 13 us: normalize(): lower_factor = jnp.linalg.cholesky(gram_matrix)]
    pallas_call x0 -> x7, Pallas kernels: none -> 18.1 us  [the longest x1 4.87 us: partial_of(): pl.pallas_call(partial_body, in_specs=[SCALAR, FAR_MEMORY, FAR_MEMORY, FA...]
  transfers between devices with their start and end apart: 5 -> 3, of which waited for: 5 -> 1; matrix products, arithmetic and copies ran while one was open for 1% -> 0% of each run, Pallas kernels for 0% -> 5%
where the time goes in v2:
time: 139 us; the launch traced here: 138 us
  blocking collectives  117 us (84%)
  Pallas kernels  18.1 us (13%)
    all_to_all x6, blocking collectives, exchange(): return lax.all_to_all(value, axes, 0, 0, tiled=True)  117 us
    pallas_call x1, Pallas kernels, partial_of(): pl.pallas_call(partial_body, in_specs=[SCALAR, FAR_MEMORY, FAR_MEMORY, FA...  4.87 us
    pallas_call x1, Pallas kernels, right_of(): pl.pallas_call(body, in_specs=[WHOLE, WHOLE, WHOLE], out_specs=[WHOLE, WH...  4.25 us
    pallas_call x1, Pallas kernels, finish(): pl.pallas_call(finish_body, grid=(layers, steps), in_specs=[pl.BlockSpec(...  2.87 us
  transfers between devices with their start and end apart: 3, of which 1 were waited for; matrix products, arithmetic and copies ran while one was open for 0% of the time, Pallas kernels for 5%

profile of v2, /device:TPU:8, one launch (start us, length us, event | category | flops | bytes accessed | tf_op | source)
XLA Modules:
  0.0 138.2 jit_solution(531155411349804051)
XLA Ops:
  0.6 1.5 %half.1 = bf16[2,128,3584]{2,1,0:T(8,128)(2,1)S(1)} custom-call(s32[1]{0:T(128)} %bitcast.core_ref, bf16[2,128,7168]{2,1,0:T(8,128)(2,1)} %x_ref.3), custom_call_target="tpu_custom_call" | custom-call | tf_op jit(solution)/shard_map/half/pallas_call | solution.py:47
  2.2 0.1 collective-permute-start
  2.3 4.9 %partial.1 = (bf16[2,64,256]{2,1,0:T(8,128)(2,1)S(1)}, bf16[2,128,3584]{2,1,0:T(8,128)(2,1)S(1)}) custom-call(s32[1]{0:T(128)} %bitcast.core_ref, bf16[2,256,5120]{2,1,0:T(8,128)(2,1)} %grad_ref.2, f32[2,64,5120]{2,1,0:T(8,128)} %bitcast.13, bf16[2,128,7168]{2,1,0:T(8,128)(2,1)} %x_ref.3), custom_call_target="tpu_custom_call" | custom-call | tf_op jit(solution)/shard_map/partial/pallas_call | solution.py:94
  7.1 0.0 copy-start
  7.1 0.6 collective-permute-start.1
  7.7 0.9 collective-permute-done.1.theirs_ref
  8.6 0.0 collective-permute-done.in_ref
  8.6 0.6 left.1
  9.3 0.0 copy-done
  9.3 23.4 %all_to_all.30 = bf16[32,112,128]{2,1,0:T(8,128)(2,1)S(1)} all-to-all(bf16[32,112,128]{2,1,0:T(8,128)(2,1)S(1)} %bitcast.11), channel_id=1, replica_groups=mesh['zh'=4,'zl'=2,'y'=4,'x'=4,'core'=2] {'zl','y','x'}, dimensions={0} | all-to-all | bytes 1835008 | tf_op jit(solution)/shard_map/all_to_all | solution.py:353
  32.7 0.1 reduce_sum.48
  32.9 16.3 %all_to_all.31 = bf16[4,112,128]{2,1,0:T(8,128)(2,1)S(1)} all-to-all(bf16[4,112,128]{2,1,0:T(8,128)(2,1)S(1)} %broadcast_in_dim.8), channel_id=1, replica_groups=mesh['zh'=4,'zl'=2,'y'=4,'x'=4,'core'=2] {'zh'}, dimensions={0} | all-to-all | bytes 229376 | tf_op jit(solution)/shard_map/all_to_all | solution.py:353
  49.2 0.0 copy-start.1
  49.2 0.1 broadcast_in_dim.9
  49.3 17.7 %all_to_all.32 = bf16[32,112,128]{2,1,0:T(8,128)(2,1)S(1)} all-to-all(bf16[32,112,128]{2,1,0:T(8,128)(2,1)S(1)} %broadcast_in_dim.9), channel_id=1, replica_groups=mesh['zh'=4,'zl'=2,'y'=4,'x'=4,'core'=2] {'zl','y','x'}, dimensions={0} | all-to-all | bytes 1835008 | tf_op jit(solution)/shard_map/all_to_all | solution.py:353
  67.0 0.0 copy-done.1
  67.0 1.4 %inner.1.refs_0_ = f32[64,640]{1,0:T(8,128)S(1)} custom-call(s32[1]{0:T(128)} %bitcast.core_ref, bf16[2,128,3584]{2,1,0:T(8,128)(2,1)S(1)} %copy-done.1, bf16[2,128,3584]{2,1,0:T(8,128)(2,1)S(1)} %collective-permute-done.in_ref, bf16[2,28,64,128]{3,2,1,0:T(8,128)(2,1)S(1)} %bitcast.8), custom_call_target="tpu_custom_call" | custom-call | tf_op jit(solution)/shard_map/inner/pallas_call | solution.py:190
  68.4 0.1 collective-permute-start.2
  68.5 2.6 %fetch.1.refs_2_ = bf16[2,256,5120]{2,1,0:T(8,128)(2,1)S(1)} custom-call(bf16[2,256,5120]{2,1,0:T(8,128)(2,1)} %grad_ref.2), custom_call_target="tpu_custom_call" | custom-call | bytes 10485760 | tf_op jit(solution)/shard_map/fetch/pallas_call | solution.py:122
  71.1 0.0 collective-permute-done.2.refs_1_
  71.1 4.2 %right.1 = (f32[2,64,64]{2,1,0:T(8,128)S(1)}, bf16[2,40,64,128]{3,2,1,0:T(8,128)(2,1)S(1)}) custom-call(f32[64,640]{1,0:T(8,128)S(1)} %inner.1.refs_0_, f32[64,640]{1,0:T(8,128)S(1)} %collective-permute-done.2.refs_1_, bf16[2,256,5120]{2,1,0:T(8,128)(2,1)S(1)} %fetch.1.refs_2_), custom_call_target="tpu_custom_call" | custom-call | tf_op jit(solution)/shard_map/right/pallas_call | solution.py:301
  75.3 25.4 %all_to_all.33 = bf16[32,160,128]{2,1,0:T(8,128)(2,1)S(1)} all-to-all(bf16[32,160,128]{2,1,0:T(8,128)(2,1)S(1)} %bitcast.12), channel_id=1, replica_groups=mesh['zh'=4,'zl'=2,'y'=4,'x'=4,'core'=2] {'x','y','zl'}, dimensions={0} | all-to-all | bytes 2621440 | tf_op jit(solution)/shard_map/all_to_all | solution.py:353
  100.8 0.2 reduce_sum.50
  101.0 11.7 %all_to_all.34 = bf16[4,160,128]{2,1,0:T(8,128)(2,1)S(1)} all-to-all(bf16[4,160,128]{2,1,0:T(8,128)(2,1)S(1)} %broadcast_in_dim.10), channel_id=1, replica_groups=mesh['zh'=4,'zl'=2,'y'=4,'x'=4,'core'=2] {'zh'}, dimensions={0} | all-to-all | bytes 327680 | tf_op jit(solution)/shard_map/all_to_all | solution.py:353
  112.7 0.2 broadcast_in_dim.11
  112.9 22.5 %all_to_all.35 = bf16[32,160,128]{2,1,0:T(8,128)(2,1)S(1)} all-to-all(bf16[32,160,128]{2,1,0:T(8,128)(2,1)S(1)} %broadcast_in_dim.11), channel_id=1, replica_groups=mesh['zh'=4,'zl'=2,'y'=4,'x'=4,'core'=2] {'x','y','zl'}, dimensions={0} | all-to-all | bytes 2621440 | tf_op jit(solution)/shard_map/all_to_all | solution.py:353
  135.4 2.9 %finish.1 = (f32[2,64,3584]{2,1,0:T(8,128)}, f32[2,64,5120]{2,1,0:T(8,128)}) custom-call(f32[2,64,64]{2,1,0:T(8,128)S(1)} %get-tuple-element.14.inverse_ref, bf16[2,28,64,128]{3,2,1,0:T(8,128)(2,1)S(1)} %bitcast.9, bf16[2,40,64,128]{3,2,1,0:T(8,128)(2,1)S(1)} %bitcast.10), custom_call_target="tpu_custom_call" | custom-call | tf_op jit(solution)/shard_map/finish/pallas_call | solution.py:331
  (4 shorter events, 0.1 us)
Async XLA Ops:
  2.2 6.5 %collective-permute-start = (bf16[2,128,3584]{2,1,0:T(8,128)(2,1)S(1)}, bf16[2,128,3584]{2,1,0:T(8,128)(2,1)S(1)}, u32[]{:S(2)}, u32[]{:S(2)}) collective-permute-start(bf16[2,128,3584]{2,1,0:T(8,128)(2,1)S(1)} %half.1), channel_id=1, source_target_pairs={{0,1},{1,0},{2,3},{3,2},{4,5},{5,4},{6,7},{7,6},{8,9},{9,8},{10,11... | collective-permute-start | bytes 5505032 | tf_op jit(solution)/shard_map/ppermute | solution.py:34
  7.1 2.2 %copy-start = (bf16[2,128,3584]{2,1,0:T(8,128)(2,1)}, bf16[2,128,3584]{2,1,0:T(8,128)(2,1)S(1)}, u32[]{:S(2)}) copy-start(bf16[2,128,3584]{2,1,0:T(8,128)(2,1)S(1)} %get-tuple-element.10.own_ref) | copy-start | bytes 5505028
  7.1 1.5 %collective-permute-start.1 = (bf16[2,64,256]{2,1,0:T(8,128)(2,1)S(1)}, bf16[2,64,256]{2,1,0:T(8,128)(2,1)S(1)}, u32[]{:S(2)}, u32[]{:S(2)}) collective-permute-start(bf16[2,64,256]{2,1,0:T(8,128)(2,1)S(1)} %get-tuple-element.11.mine_ref), channel_id=1, source_target_pairs={{0,1},{1,0},{2,3},{3,2},{4,5},{5,4},{6,7},{7,6},{8,9},{9,8},{10,11... | collective-permute-start | bytes 196616 | tf_op jit(solution)/shard_map/ppermute | solution.py:34
  49.2 17.8 %copy-start.1 = (bf16[2,128,3584]{2,1,0:T(8,128)(2,1)S(1)}, bf16[2,128,3584]{2,1,0:T(8,128)(2,1)}, u32[]{:S(2)}) copy-start(bf16[2,128,3584]{2,1,0:T(8,128)(2,1)} %copy-done) | copy-start | bytes 5505028
  68.4 2.6 %collective-permute-start.2 = (f32[64,640]{1,0:T(8,128)S(1)}, f32[64,640]{1,0:T(8,128)S(1)}, u32[]{:S(2)}, u32[]{:S(2)}) collective-permute-start(f32[64,640]{1,0:T(8,128)S(1)} %inner.1.refs_0_), channel_id=1, source_target_pairs={{0,1},{1,0},{2,3},{3,2},{4,5},{5,4},{6,7},{7,6},{8,9},{9,8},{10,11... | collective-permute-start | bytes 491528 | tf_op jit(solution)/shard_map/ppermute | solution.py:34

commit v3 on v2

--- a/solution.py
+++ b/solution.py
@@ -169,29 +169,49 @@
     )(core, near(x_own), near(x_in), near(mine), near(theirs))
 
 
+def rows_of(p_ref, layer):
+    return jnp.concatenate([p_ref[layer, tile] for tile in range(p_ref.shape[1])], axis=1)
+
+
+def gram_body(p_ref, out_ref):
+    rank = p_ref.shape[2]
+    for l in range(p_ref.shape[0]):
+        rows = rows_of(p_ref, l)
+        got = lax.dot_general(rows, rows, TRANSPOSED, preferred_element_type=F32)
+        out_ref[:, l * rank : (l + 1) * rank] = got
+
+
+def gram_of(p_blocks):
+    layers, _, rank, _ = p_blocks.shape
+    return pl.pallas_call(
+        gram_body,
+        in_specs=[WHOLE],
+        out_specs=WHOLE,
+        out_shape=pltpu.VMEM((rank, layers * rank), F32),
+        cost_estimate=pl.CostEstimate(flops=2 * rank * p_blocks.size, bytes_accessed=2 * p_blocks.size, transcendentals=0),
+        compiler_params=params(8),
+        name="gram",
+    )(near(p_blocks))
+
+
 def inner_body(core_ref, own_ref, in_ref, p_ref, out_ref):
     core = core_ref[0]
-    layers, tiles, rank, _ = p_ref.shape
     tokens = 2 * own_ref.shape[1]
-    base = layers * tokens
-    for l in range(layers):
-        rows = jnp.concatenate([p_ref[l, tile] for tile in range(tiles)], axis=1)
+    for l in range(p_ref.shape[0]):
         seen = jnp.concatenate([own_ref[l], in_ref[l]], axis=0)
-        got = lax.dot_general(rows, seen, TRANSPOSED, preferred_element_type=F32)
+        got = lax.dot_general(rows_of(p_ref, l), seen, TRANSPOSED, preferred_element_type=F32)
         out_ref[:, l * tokens : (l + 1) * tokens] = own_first(core, got)
-        got = lax.dot_general(rows, rows, TRANSPOSED, preferred_element_type=F32)
-        out_ref[:, base + l * rank : base + (l + 1) * rank] = got
 
 
 def inner_of(core, x_own, x_in, p_blocks):
-    layers, tokens, _ = x_in.shape
+    layers, tokens, half = x_in.shape
     rank = p_blocks.shape[2]
-    width = layers * (2 * tokens + rank)
     return pl.pallas_call(
         inner_body,
         in_specs=[SCALAR, WHOLE, WHOLE, WHOLE],
         out_specs=WHOLE,
-        out_shape=pltpu.VMEM((rank, width), F32),
+        out_shape=pltpu.VMEM((rank, 2 * layers * tokens), F32),
+        cost_estimate=pl.CostEstimate(flops=4 * rank * x_in.size, bytes_accessed=6 * x_in.size, transcendentals=0),
         compiler_params=params(8),
         name="inner",
     )(core, near(x_own), near(x_in), near(p_blocks))
@@ -266,21 +286,37 @@
     return high, mid, (rest - mid.astype(F32)).astype(BF16)
 
 
-def right_body(scale, mine_ref, theirs_ref, grad_ref, inverse_ref, out_ref):
-    layers, tokens, hidden = grad_ref.shape
-    rank = mine_ref.shape[0]
+def factor_body(mine_ref, theirs_ref, inverse_ref):
+    layers, rank, _ = inverse_ref.shape
     total = mine_ref[...] + theirs_ref[...]
-    base = layers * tokens
 
     def store(layer, row, value):
         inverse_ref[layer, row : row + 1, :] = value
 
-    inverse_factors([total[:, base + l * rank : base + (l + 1) * rank] for l in range(layers)], store)
+    inverse_factors([total[:, l * rank : (l + 1) * rank] for l in range(layers)], store)
+
+
+def factor_of(mine, theirs):
+    rank, width = mine.shape
+    return pl.pallas_call(
+        factor_body,
+        in_specs=[WHOLE, WHOLE],
+        out_specs=WHOLE,
+        out_shape=pltpu.VMEM((width // rank, rank, rank), F32),
+        cost_estimate=pl.CostEstimate(flops=10**9, bytes_accessed=10**6, transcendentals=0),
+        compiler_params=params(8),
+        name="factor",
+    )(near(mine), near(theirs))
+
+
+def right_body(scale, inverse_ref, mine_ref, theirs_ref, grad_ref, out_ref):
+    layers, tokens, hidden = grad_ref.shape
     wide = 2 * LANES
     for l in range(layers):
+        at = slice(l * tokens, (l + 1) * tokens)
         left = jnp.dot(
             inverse_ref[l],
-            total[:, l * tokens : (l + 1) * tokens],
+            mine_ref[:, at] + theirs_ref[:, at],
             precision=lax.Precision.HIGHEST,
             preferred_element_type=F32,
         ).astype(BF16)
@@ -291,7 +327,7 @@
             out_ref[l, 2 * tile + 1] = got[:, LANES:]
 
 
-def right_of(mine, theirs, grad, scale):
+def right_of(inverse, mine, theirs, grad, scale):
     layers, _, hidden = grad.shape
     rank, _ = mine.shape
 
@@ -300,15 +336,12 @@
 
     return pl.pallas_call(
         body,
-        in_specs=[WHOLE, WHOLE, WHOLE],
-        out_specs=[WHOLE, WHOLE],
-        out_shape=[
-            pltpu.VMEM((layers, rank, rank), F32),
-            pltpu.VMEM((layers, hidden // LANES, rank, LANES), BF16),
-        ],
+        in_specs=[WHOLE, WHOLE, WHOLE, WHOLE],
+        out_specs=WHOLE,
+        out_shape=pltpu.VMEM((layers, hidden // LANES, rank, LANES), BF16),
         compiler_params=params(8),
         name="right",
-    )(near(mine), near(theirs), near(grad))
+    )(near(inverse), near(mine), near(theirs), near(grad))
 
 
 def finish_body(inverse_ref, p_ref, q_ref, hat_ref, new_ref):
@@ -379,9 +412,12 @@
     mine, x_own = partial_of(core_array, grad_pre, jnp.swapaxes(q_prev, 1, 2), x_saved)
     theirs = swap(mine)
     p_blocks = sum_over_chips(left_of(core_array, x_own, x_in, mine, theirs), P_NEAR)
+    gram = gram_of(p_blocks)
+    grad, gram = lax.optimization_barrier((grad_pre, gram))
     inner = inner_of(core_array, x_own, x_in, p_blocks)
-    grad, tied = lax.optimization_barrier((grad_pre, inner))
-    inverse, q_blocks = right_of(tied, swap(tied), fetch(grad), scale)
+    held = fetch(grad)
+    inverse = factor_of(gram, swap(gram))
+    q_blocks = right_of(inverse, inner, swap(inner), held, scale)
     p_hat, q_new = finish(inverse, p_blocks, sum_over_chips(q_blocks, Q_NEAR))
     return jnp.swapaxes(p_hat, 1, 2), jnp.swapaxes(q_new, 1, 2)
 

time: 139 us -> 138 us (level)
  blocking collectives: 117 us -> 115 us
    all_to_all x6, blocking collectives: 117 us -> 115 us  [exchange(): return lax.all_to_all(value, axes, 0, 0, tiled=True)]
    pallas_call x1 -> x3, Pallas kernels: 4.25 us -> 4.66 us  [the longest x1 2.74 us: factor_of(): pl.pallas_call(factor_body, in_specs=[WHOLE, WHOLE], out_specs=WHOLE, out...]
  transfers between devices with their start and end apart: 3 -> 4, of which waited for: 1 -> 1; matrix products, arithmetic and copies ran while one was open for 0% -> 0% of each run, Pallas kernels for 5% -> 8%
where the time goes in v3:
time: 138 us; the launch traced here: 137 us
  blocking collectives  115 us (83%)
  Pallas kernels  18.3 us (13%)
    all_to_all x6, blocking collectives, exchange(): return lax.all_to_all(value, axes, 0, 0, tiled=True)  115 us
    pallas_call x1, Pallas kernels, partial_of(): pl.pallas_call(partial_body, in_specs=[SCALAR, FAR_MEMORY, FAR_MEMORY, FA...  4.87 us
    pallas_call x1, Pallas kernels, finish(): pl.pallas_call(finish_body, grid=(layers, steps), in_specs=[pl.BlockSpec(...  2.87 us
  transfers between devices with their start and end apart: 4, of which 1 were waited for; matrix products, arithmetic and copies ran while one was open for 0% of the time, Pallas kernels for 8%

profile of v3, /device:TPU:8, one launch (start us, length us, event | category | flops | bytes accessed | tf_op | source)
XLA Modules:
  0.0 137.4 jit_solution(13505983253864355330)
XLA Ops:
  0.6 1.5 %half.1 = bf16[2,128,3584]{2,1,0:T(8,128)(2,1)S(1)} custom-call(s32[1]{0:T(128)} %bitcast.core_ref, bf16[2,128,7168]{2,1,0:T(8,128)(2,1)} %x_ref.3), custom_call_target="tpu_custom_call" | custom-call | tf_op jit(solution)/shard_map/half/pallas_call | solution.py:47
  2.2 0.1 collective-permute-start
  2.3 4.9 %partial.1 = (bf16[2,64,256]{2,1,0:T(8,128)(2,1)S(1)}, bf16[2,128,3584]{2,1,0:T(8,128)(2,1)S(1)}) custom-call(s32[1]{0:T(128)} %bitcast.core_ref, bf16[2,256,5120]{2,1,0:T(8,128)(2,1)} %grad_ref.2, f32[2,64,5120]{2,1,0:T(8,128)} %bitcast.14, bf16[2,128,7168]{2,1,0:T(8,128)(2,1)} %x_ref.3), custom_call_target="tpu_custom_call" | custom-call | tf_op jit(solution)/shard_map/partial/pallas_call | solution.py:94
  7.1 0.0 copy-start
  7.1 0.6 collective-permute-start.1
  7.7 0.9 collective-permute-done.1.theirs_ref
  8.6 0.0 collective-permute-done.in_ref
  8.6 0.6 left.1
  9.3 0.0 copy-done
  9.3 23.4 %all_to_all.30 = bf16[32,112,128]{2,1,0:T(8,128)(2,1)S(1)} all-to-all(bf16[32,112,128]{2,1,0:T(8,128)(2,1)S(1)} %bitcast.13), channel_id=1, replica_groups=mesh['zh'=4,'zl'=2,'y'=4,'x'=4,'core'=2] {'zl','y','x'}, dimensions={0} | all-to-all | bytes 1835008 | tf_op jit(solution)/shard_map/all_to_all | solution.py:386
  32.7 0.1 reduce_sum.48
  32.9 16.3 %all_to_all.31 = bf16[4,112,128]{2,1,0:T(8,128)(2,1)S(1)} all-to-all(bf16[4,112,128]{2,1,0:T(8,128)(2,1)S(1)} %broadcast_in_dim.8), channel_id=1, replica_groups=mesh['zh'=4,'zl'=2,'y'=4,'x'=4,'core'=2] {'zh'}, dimensions={0} | all-to-all | bytes 229376 | tf_op jit(solution)/shard_map/all_to_all | solution.py:386
  49.2 0.0 copy-start.1
  49.2 0.1 broadcast_in_dim.9
  49.3 17.7 %all_to_all.32 = bf16[32,112,128]{2,1,0:T(8,128)(2,1)S(1)} all-to-all(bf16[32,112,128]{2,1,0:T(8,128)(2,1)S(1)} %broadcast_in_dim.9), channel_id=1, replica_groups=mesh['zh'=4,'zl'=2,'y'=4,'x'=4,'core'=2] {'zl','y','x'}, dimensions={0} | all-to-all | bytes 1835008 | tf_op jit(solution)/shard_map/all_to_all | solution.py:386
  67.0 0.0 copy-done.1
  67.0 1.2 inner.1.refs_1_
  68.2 0.1 collective-permute-start.3
  68.3 0.4 gram.1.mine_ref
  68.8 0.6 collective-permute-start.2
  69.3 2.5 %fetch.1.refs_3_ = bf16[2,256,5120]{2,1,0:T(8,128)(2,1)S(1)} custom-call(bf16[2,256,5120]{2,1,0:T(8,128)(2,1)} %grad_ref.2), custom_call_target="tpu_custom_call" | custom-call | bytes 10485760 | tf_op jit(solution)/shard_map/fetch/pallas_call | solution.py:122
  71.9 0.0 collective-permute-done.2.theirs_ref
  71.9 2.7 %factor.1.refs_0_.inverse_ref = f32[2,64,64]{2,1,0:T(8,128)S(1)} custom-call(f32[64,128]{1,0:T(8,128)S(1)} %gram.1.mine_ref, f32[64,128]{1,0:T(8,128)S(1)} %collective-permute-done.2.theirs_ref), custom_call_target="tpu_custom_call" | custom-call | flops 1000000000 | bytes 1000000 | tf_op jit(solution)/shard_map/factor/pallas_call | solution.py:301
  74.6 0.0 collective-permute-done.3.refs_2_
  74.6 1.5 %right.1 = bf16[2,40,64,128]{3,2,1,0:T(8,128)(2,1)S(1)} custom-call(f32[2,64,64]{2,1,0:T(8,128)S(1)} %factor.1.refs_0_.inverse_ref, f32[64,512]{1,0:T(8,128)S(1)} %inner.1.refs_1_, f32[64,512]{1,0:T(8,128)S(1)} %collective-permute-done.3.refs_2_, bf16[2,256,5120]{2,1,0:T(8,128)(2,1)S(1)} %fetch.1.refs_3_), custom_call_target="tpu_custom_call" | custom-call | tf_op jit(solution)/shard_map/right/pallas_call | solution.py:337
  76.1 25.1 %all_to_all.33 = bf16[32,160,128]{2,1,0:T(8,128)(2,1)S(1)} all-to-all(bf16[32,160,128]{2,1,0:T(8,128)(2,1)S(1)} %bitcast.12), channel_id=1, replica_groups=mesh['zh'=4,'zl'=2,'y'=4,'x'=4,'core'=2] {'x','y','zl'}, dimensions={0} | all-to-all | bytes 2621440 | tf_op jit(solution)/shard_map/all_to_all | solution.py:386
  101.2 0.2 reduce_sum.50
  101.4 10.9 %all_to_all.34 = bf16[4,160,128]{2,1,0:T(8,128)(2,1)S(1)} all-to-all(bf16[4,160,128]{2,1,0:T(8,128)(2,1)S(1)} %broadcast_in_dim.10), channel_id=1, replica_groups=mesh['zh'=4,'zl'=2,'y'=4,'x'=4,'core'=2] {'zh'}, dimensions={0} | all-to-all | bytes 327680 | tf_op jit(solution)/shard_map/all_to_all | solution.py:386
  112.4 0.2 broadcast_in_dim.11
  112.5 22.0 %all_to_all.35 = bf16[32,160,128]{2,1,0:T(8,128)(2,1)S(1)} all-to-all(bf16[32,160,128]{2,1,0:T(8,128)(2,1)S(1)} %broadcast_in_dim.11), channel_id=1, replica_groups=mesh['zh'=4,'zl'=2,'y'=4,'x'=4,'core'=2] {'x','y','zl'}, dimensions={0} | all-to-all | bytes 2621440 | tf_op jit(solution)/shard_map/all_to_all | solution.py:386
  134.6 2.9 %finish.1 = (f32[2,64,3584]{2,1,0:T(8,128)}, f32[2,64,5120]{2,1,0:T(8,128)}) custom-call(f32[2,64,64]{2,1,0:T(8,128)S(1)} %factor.1.refs_0_.inverse_ref, bf16[2,28,64,128]{3,2,1,0:T(8,128)(2,1)S(1)} %bitcast.10, bf16[2,40,64,128]{3,2,1,0:T(8,128)(2,1)S(1)} %bitcast.11), custom_call_target="tpu_custom_call" | custom-call | tf_op jit(solution)/shard_map/finish/pallas_call | solution.py:364
  (4 shorter events, 0.1 us)
Async XLA Ops:
  2.2 6.5 %collective-permute-start = (bf16[2,128,3584]{2,1,0:T(8,128)(2,1)S(1)}, bf16[2,128,3584]{2,1,0:T(8,128)(2,1)S(1)}, u32[]{:S(2)}, u32[]{:S(2)}) collective-permute-start(bf16[2,128,3584]{2,1,0:T(8,128)(2,1)S(1)} %half.1), channel_id=1, source_target_pairs={{0,1},{1,0},{2,3},{3,2},{4,5},{5,4},{6,7},{7,6},{8,9},{9,8},{10,11... | collective-permute-start | bytes 5505032 | tf_op jit(solution)/shard_map/ppermute | solution.py:34
  7.1 2.2 %copy-start = (bf16[2,128,3584]{2,1,0:T(8,128)(2,1)}, bf16[2,128,3584]{2,1,0:T(8,128)(2,1)S(1)}, u32[]{:S(2)}) copy-start(bf16[2,128,3584]{2,1,0:T(8,128)(2,1)S(1)} %get-tuple-element.8.own_ref) | copy-start | bytes 5505028
  7.1 1.5 %collective-permute-start.1 = (bf16[2,64,256]{2,1,0:T(8,128)(2,1)S(1)}, bf16[2,64,256]{2,1,0:T(8,128)(2,1)S(1)}, u32[]{:S(2)}, u32[]{:S(2)}) collective-permute-start(bf16[2,64,256]{2,1,0:T(8,128)(2,1)S(1)} %get-tuple-element.9.mine_ref), channel_id=1, source_target_pairs={{0,1},{1,0},{2,3},{3,2},{4,5},{5,4},{6,7},{7,6},{8,9},{9,8},{10,11... | collective-permute-start | bytes 196616 | tf_op jit(solution)/shard_map/ppermute | solution.py:34
  49.2 17.8 %copy-start.1 = (bf16[2,128,3584]{2,1,0:T(8,128)(2,1)S(1)}, bf16[2,128,3584]{2,1,0:T(8,128)(2,1)}, u32[]{:S(2)}) copy-start(bf16[2,128,3584]{2,1,0:T(8,128)(2,1)} %copy-done) | copy-start | bytes 5505028
  68.2 6.4 %collective-permute-start.3 = (f32[64,512]{1,0:T(8,128)S(1)}, f32[64,512]{1,0:T(8,128)S(1)}, u32[]{:S(2)}, u32[]{:S(2)}) collective-permute-start(f32[64,512]{1,0:T(8,128)S(1)} %inner.1.refs_1_), channel_id=1, source_target_pairs={{0,1},{1,0},{2,3},{3,2},{4,5},{5,4},{6,7},{7,6},{8,9},{9,8},{10,11... | collective-permute-start | bytes 393224 | tf_op jit(solution)/shard_map/ppermute | solution.py:34
  68.8 3.1 %collective-permute-start.2 = (f32[64,128]{1,0:T(8,128)S(1)}, f32[64,128]{1,0:T(8,128)S(1)}, u32[]{:S(2)}, u32[]{:S(2)}) collective-permute-start(f32[64,128]{1,0:T(8,128)S(1)} %gram.1.mine_ref), channel_id=1, source_target_pairs={{0,1},{1,0},{2,3},{3,2},{4,5},{5,4},{6,7},{7,6},{8,9},{9,8},{10,11... | collective-permute-start | bytes 98312 | tf_op jit(solution)/shard_map/ppermute | solution.py:34

commit v4 on v3

--- a/solution.py
+++ b/solution.py
@@ -110,12 +110,10 @@
     )(core, stay(grad), stay(q_rows), stay(x))
 
 
-def fetch_body(grad_ref, out_ref, sems):
-    moves = [pltpu.make_async_copy(grad_ref.at[l], out_ref.at[l], sems.at[l]) for l in range(out_ref.shape[0])]
-    for move in moves:
-        move.start()
-    for move in moves:
-        move.wait()
+def fetch_body(grad_ref, out_ref, sem):
+    move = pltpu.make_async_copy(grad_ref.at[0], out_ref, sem)
+    move.start()
+    move.wait()
 
 
 def fetch(grad):
@@ -123,9 +121,9 @@
         fetch_body,
         in_specs=[FAR_MEMORY],
         out_specs=WHOLE,
-        out_shape=pltpu.VMEM(grad.shape, BF16),
-        scratch_shapes=[pltpu.SemaphoreType.DMA((grad.shape[0],))],
-        cost_estimate=pl.CostEstimate(flops=0, bytes_accessed=4 * grad.size, transcendentals=0),
+        out_shape=pltpu.VMEM(grad.shape[1:], BF16),
+        scratch_shapes=[pltpu.SemaphoreType.DMA],
+        cost_estimate=pl.CostEstimate(flops=0, bytes_accessed=2 * grad.size, transcendentals=0),
         compiler_params=params(4),
         name="fetch",
     )(stay(grad))
@@ -309,9 +307,12 @@
     )(near(mine), near(theirs))
 
 
-def right_body(scale, inverse_ref, mine_ref, theirs_ref, grad_ref, out_ref):
+def right_body(scale, inverse_ref, mine_ref, theirs_ref, first_ref, grad_ref, out_ref, held, sems):
     layers, tokens, hidden = grad_ref.shape
     wide = 2 * LANES
+    moves = [pltpu.make_async_copy(grad_ref.at[l], held.at[l - 1], sems.at[l - 1]) for l in range(1, layers)]
+    for move in moves:
+        move.start()
     for l in range(layers):
         at = slice(l * tokens, (l + 1) * tokens)
         left = jnp.dot(
@@ -320,15 +321,19 @@
             precision=lax.Precision.HIGHEST,
             preferred_element_type=F32,
         ).astype(BF16)
+        if l > 0:
+            moves[l - 1].wait()
         for tile in range(hidden // wide):
-            got = jnp.dot(left, grad_ref[l, :, tile * wide : (tile + 1) * wide], preferred_element_type=F32)
+            cut = slice(tile * wide, (tile + 1) * wide)
+            rows = first_ref[:, cut] if l == 0 else held[l - 1, :, cut]
+            got = jnp.dot(left, rows, preferred_element_type=F32)
             got = (got * scale).astype(BF16)
             out_ref[l, 2 * tile] = got[:, :LANES]
             out_ref[l, 2 * tile + 1] = got[:, LANES:]
 
 
-def right_of(inverse, mine, theirs, grad, scale):
-    layers, _, hidden = grad.shape
+def right_of(inverse, mine, theirs, first, grad, scale):
+    layers, tokens, hidden = grad.shape
     rank, _ = mine.shape
 
     def body(*refs):
@@ -336,12 +341,13 @@
 
     return pl.pallas_call(
         body,
-        in_specs=[WHOLE, WHOLE, WHOLE, WHOLE],
+        in_specs=[WHOLE, WHOLE, WHOLE, WHOLE, FAR_MEMORY],
         out_specs=WHOLE,
         out_shape=pltpu.VMEM((layers, hidden // LANES, rank, LANES), BF16),
-        compiler_params=params(8),
+        scratch_shapes=[pltpu.VMEM((layers - 1, tokens, hidden), BF16), pltpu.SemaphoreType.DMA((layers - 1,))],
+        compiler_params=params(10),
         name="right",
-    )(near(inverse), near(mine), near(theirs), near(grad))
+    )(near(inverse), near(mine), near(theirs), near(first), stay(grad))
 
 
 def finish_body(inverse_ref, p_ref, q_ref, hat_ref, new_ref):
@@ -415,9 +421,9 @@
     gram = gram_of(p_blocks)
     grad, gram = lax.optimization_barrier((grad_pre, gram))
     inner = inner_of(core_array, x_own, x_in, p_blocks)
-    held = fetch(grad)
+    first = fetch(grad)
     inverse = factor_of(gram, swap(gram))
-    q_blocks = right_of(inverse, inner, swap(inner), held, scale)
+    q_blocks = right_of(inverse, inner, swap(inner), first, grad, scale)
     p_hat, q_new = finish(inverse, p_blocks, sum_over_chips(q_blocks, Q_NEAR))
     return jnp.swapaxes(p_hat, 1, 2), jnp.swapaxes(q_new, 1, 2)
 

time: 138 us -> 138 us (level)
  transfers between devices with their start and end apart: 4 -> 4, of which waited for: 1 -> 1; matrix products, arithmetic and copies ran while one was open for 0% -> 0% of each run, Pallas kernels for 8% -> 7%
where the time goes in v4:
time: 138 us
  blocking collectives  115 us (83%)
  Pallas kernels  18.4 us (13%)
    all_to_all x6, blocking collectives, exchange(): return lax.all_to_all(value, axes, 0, 0, tiled=True)  115 us
    pallas_call x1, Pallas kernels, partial_of(): pl.pallas_call(partial_body, in_specs=[SCALAR, FAR_MEMORY, FAR_MEMORY, FA...  4.87 us
    pallas_call x1, Pallas kernels, finish(): pl.pallas_call(finish_body, grid=(layers, steps), in_specs=[pl.BlockSpec(...  2.87 us
  transfers between devices with their start and end apart: 4, of which 1 were waited for; matrix products, arithmetic and copies ran while one was open for 0% of the time, Pallas kernels for 7%

profile of v4, /device:TPU:8, one launch (start us, length us, event | category | flops | bytes accessed | tf_op | source)
XLA Modules:
  0.0 137.5 jit_solution(16691360539047542116)
XLA Ops:
  0.6 1.5 %half.1 = bf16[2,128,3584]{2,1,0:T(8,128)(2,1)S(1)} custom-call(s32[1]{0:T(128)} %bitcast.core_ref, bf16[2,128,7168]{2,1,0:T(8,128)(2,1)} %x_ref.3), custom_call_target="tpu_custom_call" | custom-call | tf_op jit(solution)/shard_map/half/pallas_call | solution.py:47
  2.2 0.1 collective-permute-start
  2.3 4.9 %partial.1 = (bf16[2,64,256]{2,1,0:T(8,128)(2,1)S(1)}, bf16[2,128,3584]{2,1,0:T(8,128)(2,1)S(1)}) custom-call(s32[1]{0:T(128)} %bitcast.core_ref, bf16[2,256,5120]{2,1,0:T(8,128)(2,1)} %refs_4_, f32[2,64,5120]{2,1,0:T(8,128)} %bitcast.14, bf16[2,128,7168]{2,1,0:T(8,128)(2,1)} %x_ref.3), custom_call_target="tpu_custom_call" | custom-call | tf_op jit(solution)/shard_map/partial/pallas_call | solution.py:94
  7.1 0.0 copy-start
  7.1 0.6 collective-permute-start.1
  7.7 0.9 collective-permute-done.1.theirs_ref
  8.6 0.0 collective-permute-done.in_ref
  8.6 0.6 left.1
  9.3 0.0 copy-done
  9.3 23.4 %all_to_all.30 = bf16[32,112,128]{2,1,0:T(8,128)(2,1)S(1)} all-to-all(bf16[32,112,128]{2,1,0:T(8,128)(2,1)S(1)} %bitcast.13), channel_id=1, replica_groups=mesh['zh'=4,'zl'=2,'y'=4,'x'=4,'core'=2] {'zl','y','x'}, dimensions={0} | all-to-all | bytes 1835008 | tf_op jit(solution)/shard_map/all_to_all | solution.py:392
  32.7 0.1 reduce_sum.48
  32.9 16.3 %all_to_all.31 = bf16[4,112,128]{2,1,0:T(8,128)(2,1)S(1)} all-to-all(bf16[4,112,128]{2,1,0:T(8,128)(2,1)S(1)} %broadcast_in_dim.8), channel_id=1, replica_groups=mesh['zh'=4,'zl'=2,'y'=4,'x'=4,'core'=2] {'zh'}, dimensions={0} | all-to-all | bytes 229376 | tf_op jit(solution)/shard_map/all_to_all | solution.py:392
  49.2 0.0 copy-start.1
  49.2 0.1 broadcast_in_dim.9
  49.3 17.7 %all_to_all.32 = bf16[32,112,128]{2,1,0:T(8,128)(2,1)S(1)} all-to-all(bf16[32,112,128]{2,1,0:T(8,128)(2,1)S(1)} %broadcast_in_dim.9), channel_id=1, replica_groups=mesh['zh'=4,'zl'=2,'y'=4,'x'=4,'core'=2] {'zl','y','x'}, dimensions={0} | all-to-all | bytes 1835008 | tf_op jit(solution)/shard_map/all_to_all | solution.py:392
  67.0 0.0 copy-done.1
  67.0 1.2 inner.1.refs_1_
  68.2 0.1 collective-permute-start.3
  68.3 0.4 gram.1.mine_ref
  68.8 0.6 collective-permute-start.2
  69.3 1.7 %fetch.1.refs_3_ = bf16[256,5120]{1,0:T(8,128)(2,1)S(1)} custom-call(bf16[2,256,5120]{2,1,0:T(8,128)(2,1)} %refs_4_), custom_call_target="tpu_custom_call" | custom-call | bytes 5242880 | tf_op jit(solution)/shard_map/fetch/pallas_call | solution.py:120
  71.1 0.0 collective-permute-done.2.theirs_ref
  71.1 2.7 %factor.1.refs_0_.inverse_ref = f32[2,64,64]{2,1,0:T(8,128)S(1)} custom-call(f32[64,128]{1,0:T(8,128)S(1)} %gram.1.mine_ref, f32[64,128]{1,0:T(8,128)S(1)} %collective-permute-done.2.theirs_ref), custom_call_target="tpu_custom_call" | custom-call | flops 1000000000 | bytes 1000000 | tf_op jit(solution)/shard_map/factor/pallas_call | solution.py:299
  73.8 0.0 collective-permute-done.3.refs_2_
  73.8 2.4 %right.1 = bf16[2,40,64,128]{3,2,1,0:T(8,128)(2,1)S(1)} custom-call(f32[2,64,64]{2,1,0:T(8,128)S(1)} %factor.1.refs_0_.inverse_ref, f32[64,512]{1,0:T(8,128)S(1)} %inner.1.refs_1_, f32[64,512]{1,0:T(8,128)S(1)} %collective-permute-done.3.refs_2_, bf16[256,5120]{1,0:T(8,128)(2,1)S(1)} %fetch.1.refs_3_, bf16[2,256,5120]{2,1,0:T(8,128)(2,1)} %refs_4_), custom_call_target="tpu_custom_call" | custom-call | tf_op jit(solution)/shard_map/right/pallas_call | solution.py:342
  76.2 25.1 %all_to_all.33 = bf16[32,160,128]{2,1,0:T(8,128)(2,1)S(1)} all-to-all(bf16[32,160,128]{2,1,0:T(8,128)(2,1)S(1)} %bitcast.11), channel_id=1, replica_groups=mesh['zh'=4,'zl'=2,'y'=4,'x'=4,'core'=2] {'x','y','zl'}, dimensions={0} | all-to-all | bytes 2621440 | tf_op jit(solution)/shard_map/all_to_all | solution.py:392
  101.3 0.2 reduce_sum.50
  101.5 10.9 %all_to_all.34 = bf16[4,160,128]{2,1,0:T(8,128)(2,1)S(1)} all-to-all(bf16[4,160,128]{2,1,0:T(8,128)(2,1)S(1)} %broadcast_in_dim.10), channel_id=1, replica_groups=mesh['zh'=4,'zl'=2,'y'=4,'x'=4,'core'=2] {'zh'}, dimensions={0} | all-to-all | bytes 327680 | tf_op jit(solution)/shard_map/all_to_all | solution.py:392
  112.4 0.2 broadcast_in_dim.11
  112.6 22.0 %all_to_all.35 = bf16[32,160,128]{2,1,0:T(8,128)(2,1)S(1)} all-to-all(bf16[32,160,128]{2,1,0:T(8,128)(2,1)S(1)} %broadcast_in_dim.11), channel_id=1, replica_groups=mesh['zh'=4,'zl'=2,'y'=4,'x'=4,'core'=2] {'x','y','zl'}, dimensions={0} | all-to-all | bytes 2621440 | tf_op jit(solution)/shard_map/all_to_all | solution.py:392
  134.6 2.9 %finish.1 = (f32[2,64,3584]{2,1,0:T(8,128)}, f32[2,64,5120]{2,1,0:T(8,128)}) custom-call(f32[2,64,64]{2,1,0:T(8,128)S(1)} %factor.1.refs_0_.inverse_ref, bf16[2,28,64,128]{3,2,1,0:T(8,128)(2,1)S(1)} %bitcast.10, bf16[2,40,64,128]{3,2,1,0:T(8,128)(2,1)S(1)} %bitcast.12), custom_call_target="tpu_custom_call" | custom-call | tf_op jit(solution)/shard_map/finish/pallas_call | solution.py:370
  (4 shorter events, 0.1 us)
Async XLA Ops:
  2.2 6.5 %collective-permute-start = (bf16[2,128,3584]{2,1,0:T(8,128)(2,1)S(1)}, bf16[2,128,3584]{2,1,0:T(8,128)(2,1)S(1)}, u32[]{:S(2)}, u32[]{:S(2)}) collective-permute-start(bf16[2,128,3584]{2,1,0:T(8,128)(2,1)S(1)} %half.1), channel_id=1, source_target_pairs={{0,1},{1,0},{2,3},{3,2},{4,5},{5,4},{6,7},{7,6},{8,9},{9,8},{10,11... | collective-permute-start | bytes 5505032 | tf_op jit(solution)/shard_map/ppermute | solution.py:34
  7.1 2.2 %copy-start = (bf16[2,128,3584]{2,1,0:T(8,128)(2,1)}, bf16[2,128,3584]{2,1,0:T(8,128)(2,1)S(1)}, u32[]{:S(2)}) copy-start(bf16[2,128,3584]{2,1,0:T(8,128)(2,1)S(1)} %get-tuple-element.8.own_ref) | copy-start | bytes 5505028
  7.1 1.5 %collective-permute-start.1 = (bf16[2,64,256]{2,1,0:T(8,128)(2,1)S(1)}, bf16[2,64,256]{2,1,0:T(8,128)(2,1)S(1)}, u32[]{:S(2)}, u32[]{:S(2)}) collective-permute-start(bf16[2,64,256]{2,1,0:T(8,128)(2,1)S(1)} %get-tuple-element.9.mine_ref), channel_id=1, source_target_pairs={{0,1},{1,0},{2,3},{3,2},{4,5},{5,4},{6,7},{7,6},{8,9},{9,8},{10,11... | collective-permute-start | bytes 196616 | tf_op jit(solution)/shard_map/ppermute | solution.py:34
  49.2 17.8 %copy-start.1 = (bf16[2,128,3584]{2,1,0:T(8,128)(2,1)S(1)}, bf16[2,128,3584]{2,1,0:T(8,128)(2,1)}, u32[]{:S(2)}) copy-start(bf16[2,128,3584]{2,1,0:T(8,128)(2,1)} %copy-done) | copy-start | bytes 5505028
  68.2 5.6 %collective-permute-start.3 = (f32[64,512]{1,0:T(8,128)S(1)}, f32[64,512]{1,0:T(8,128)S(1)}, u32[]{:S(2)}, u32[]{:S(2)}) collective-permute-start(f32[64,512]{1,0:T(8,128)S(1)} %inner.1.refs_1_), channel_id=1, source_target_pairs={{0,1},{1,0},{2,3},{3,2},{4,5},{5,4},{6,7},{7,6},{8,9},{9,8},{10,11... | collective-permute-start | bytes 393224 | tf_op jit(solution)/shard_map/ppermute | solution.py:34
  68.8 2.3 %collective-permute-start.2 = (f32[64,128]{1,0:T(8,128)S(1)}, f32[64,128]{1,0:T(8,128)S(1)}, u32[]{:S(2)}, u32[]{:S(2)}) collective-permute-start(f32[64,128]{1,0:T(8,128)S(1)} %gram.1.mine_ref), channel_id=1, source_target_pairs={{0,1},{1,0},{2,3},{3,2},{4,5},{5,4},{6,7},{7,6},{8,9},{9,8},{10,11... | collective-permute-start | bytes 98312 | tf_op jit(solution)/shard_map/ppermute | solution.py:34

commit v5 on v3

--- a/solution.py
+++ b/solution.py
@@ -268,15 +268,17 @@
                     factors[k, m] = value * roots[k]
             for k in range(height):
                 store(index, first + k, scaled[k][:1, rank:])
+            solved = [None] * height
+            for k in reversed(range(height)):
+                value = scaled[k]
+                for q in range(k + 1, height):
+                    value = value - factors[k, q] * solved[q]
+                solved[k] = value * roots[k]
             for b in range(at + 1, blocks):
-                lower = []
-                for k in range(height):
-                    value = columns[b][k]
-                    for q in range(k):
-                        value = value - lower[q] * factors[q, k]
-                    lower.append(value * roots[k])
-                for k in range(height):
-                    rows[b] = rows[b] - lower[k] * scaled[k]
+                terms = [columns[b][k] * solved[k] for k in range(height)]
+                while len(terms) > 1:
+                    terms = [terms[k] + terms[k + 1] for k in range(0, len(terms), 2)]
+                rows[b] = rows[b] - terms[0]
 
 
 def split3(value):

time: 138 us -> 138 us (level)
  no operation moved by 1% of the time
where the time goes in v5:
time: 138 us; the launch traced here: 137 us
  blocking collectives  115 us (83%)
  Pallas kernels  18.1 us (13%)
    all_to_all x6, blocking collectives, exchange(): return lax.all_to_all(value, axes, 0, 0, tiled=True)  115 us
    pallas_call x1, Pallas kernels, partial_of(): pl.pallas_call(partial_body, in_specs=[SCALAR, FAR_MEMORY, FAR_MEMORY, FA...  4.87 us
    pallas_call x1, Pallas kernels, finish(): pl.pallas_call(finish_body, grid=(layers, steps), in_specs=[pl.BlockSpec(...  2.87 us
  transfers between devices with their start and end apart: 4, of which 1 were waited for; matrix products, arithmetic and copies ran while one was open for 0% of the time, Pallas kernels for 8%

profile of v5, /device:TPU:8, one launch (start us, length us, event | category | flops | bytes accessed | tf_op | source)
XLA Modules:
  0.0 137.2 jit_solution(8211645121276908877)
XLA Ops:
  0.6 1.5 %half.1 = bf16[2,128,3584]{2,1,0:T(8,128)(2,1)S(1)} custom-call(s32[1]{0:T(128)} %bitcast.core_ref, bf16[2,128,7168]{2,1,0:T(8,128)(2,1)} %x_ref.3), custom_call_target="tpu_custom_call" | custom-call | tf_op jit(solution)/shard_map/half/pallas_call | solution.py:47
  2.2 0.1 collective-permute-start
  2.3 4.9 %partial.1 = (bf16[2,64,256]{2,1,0:T(8,128)(2,1)S(1)}, bf16[2,128,3584]{2,1,0:T(8,128)(2,1)S(1)}) custom-call(s32[1]{0:T(128)} %bitcast.core_ref, bf16[2,256,5120]{2,1,0:T(8,128)(2,1)} %grad_ref.2, f32[2,64,5120]{2,1,0:T(8,128)} %bitcast.14, bf16[2,128,7168]{2,1,0:T(8,128)(2,1)} %x_ref.3), custom_call_target="tpu_custom_call" | custom-call | tf_op jit(solution)/shard_map/partial/pallas_call | solution.py:94
  7.1 0.0 copy-start
  7.1 0.6 collective-permute-start.1
  7.7 0.9 collective-permute-done.1.theirs_ref
  8.6 0.0 collective-permute-done.in_ref
  8.6 0.6 left.1
  9.3 0.0 copy-done
  9.3 23.4 %all_to_all.30 = bf16[32,112,128]{2,1,0:T(8,128)(2,1)S(1)} all-to-all(bf16[32,112,128]{2,1,0:T(8,128)(2,1)S(1)} %bitcast.13), channel_id=1, replica_groups=mesh['zh'=4,'zl'=2,'y'=4,'x'=4,'core'=2] {'zl','y','x'}, dimensions={0} | all-to-all | bytes 1835008 | tf_op jit(solution)/shard_map/all_to_all | solution.py:388
  32.7 0.1 reduce_sum.48
  32.9 16.3 %all_to_all.31 = bf16[4,112,128]{2,1,0:T(8,128)(2,1)S(1)} all-to-all(bf16[4,112,128]{2,1,0:T(8,128)(2,1)S(1)} %broadcast_in_dim.8), channel_id=1, replica_groups=mesh['zh'=4,'zl'=2,'y'=4,'x'=4,'core'=2] {'zh'}, dimensions={0} | all-to-all | bytes 229376 | tf_op jit(solution)/shard_map/all_to_all | solution.py:388
  49.2 0.0 copy-start.1
  49.2 0.1 broadcast_in_dim.9
  49.3 17.7 %all_to_all.32 = bf16[32,112,128]{2,1,0:T(8,128)(2,1)S(1)} all-to-all(bf16[32,112,128]{2,1,0:T(8,128)(2,1)S(1)} %broadcast_in_dim.9), channel_id=1, replica_groups=mesh['zh'=4,'zl'=2,'y'=4,'x'=4,'core'=2] {'zl','y','x'}, dimensions={0} | all-to-all | bytes 1835008 | tf_op jit(solution)/shard_map/all_to_all | solution.py:388
  67.0 0.0 copy-done.1
  67.0 1.2 inner.1.refs_1_
  68.2 0.1 collective-permute-start.3
  68.3 0.4 gram.1.mine_ref
  68.8 0.6 collective-permute-start.2
  69.3 2.5 %fetch.1.refs_3_ = bf16[2,256,5120]{2,1,0:T(8,128)(2,1)S(1)} custom-call(bf16[2,256,5120]{2,1,0:T(8,128)(2,1)} %grad_ref.2), custom_call_target="tpu_custom_call" | custom-call | bytes 10485760 | tf_op jit(solution)/shard_map/fetch/pallas_call | solution.py:122
  71.9 0.0 collective-permute-done.2.theirs_ref
  71.9 2.5 %factor.1.refs_0_.inverse_ref = f32[2,64,64]{2,1,0:T(8,128)S(1)} custom-call(f32[64,128]{1,0:T(8,128)S(1)} %gram.1.mine_ref, f32[64,128]{1,0:T(8,128)S(1)} %collective-permute-done.2.theirs_ref), custom_call_target="tpu_custom_call" | custom-call | flops 1000000000 | bytes 1000000 | tf_op jit(solution)/shard_map/factor/pallas_call | solution.py:303
  74.4 0.0 collective-permute-done.3.refs_2_
  74.4 1.5 %right.1 = bf16[2,40,64,128]{3,2,1,0:T(8,128)(2,1)S(1)} custom-call(f32[2,64,64]{2,1,0:T(8,128)S(1)} %factor.1.refs_0_.inverse_ref, f32[64,512]{1,0:T(8,128)S(1)} %inner.1.refs_1_, f32[64,512]{1,0:T(8,128)S(1)} %collective-permute-done.3.refs_2_, bf16[2,256,5120]{2,1,0:T(8,128)(2,1)S(1)} %fetch.1.refs_3_), custom_call_target="tpu_custom_call" | custom-call | tf_op jit(solution)/shard_map/right/pallas_call | solution.py:339
  75.9 25.1 %all_to_all.33 = bf16[32,160,128]{2,1,0:T(8,128)(2,1)S(1)} all-to-all(bf16[32,160,128]{2,1,0:T(8,128)(2,1)S(1)} %bitcast.12), channel_id=1, replica_groups=mesh['zh'=4,'zl'=2,'y'=4,'x'=4,'core'=2] {'x','y','zl'}, dimensions={0} | all-to-all | bytes 2621440 | tf_op jit(solution)/shard_map/all_to_all | solution.py:388
  101.0 0.2 reduce_sum.50
  101.2 10.9 %all_to_all.34 = bf16[4,160,128]{2,1,0:T(8,128)(2,1)S(1)} all-to-all(bf16[4,160,128]{2,1,0:T(8,128)(2,1)S(1)} %broadcast_in_dim.10), channel_id=1, replica_groups=mesh['zh'=4,'zl'=2,'y'=4,'x'=4,'core'=2] {'zh'}, dimensions={0} | all-to-all | bytes 327680 | tf_op jit(solution)/shard_map/all_to_all | solution.py:388
  112.1 0.2 broadcast_in_dim.11
  112.3 22.0 %all_to_all.35 = bf16[32,160,128]{2,1,0:T(8,128)(2,1)S(1)} all-to-all(bf16[32,160,128]{2,1,0:T(8,128)(2,1)S(1)} %broadcast_in_dim.11), channel_id=1, replica_groups=mesh['zh'=4,'zl'=2,'y'=4,'x'=4,'core'=2] {'x','y','zl'}, dimensions={0} | all-to-all | bytes 2621440 | tf_op jit(solution)/shard_map/all_to_all | solution.py:388
  134.4 2.9 %finish.1 = (f32[2,64,3584]{2,1,0:T(8,128)}, f32[2,64,5120]{2,1,0:T(8,128)}) custom-call(f32[2,64,64]{2,1,0:T(8,128)S(1)} %factor.1.refs_0_.inverse_ref, bf16[2,28,64,128]{3,2,1,0:T(8,128)(2,1)S(1)} %bitcast.10, bf16[2,40,64,128]{3,2,1,0:T(8,128)(2,1)S(1)} %bitcast.11), custom_call_target="tpu_custom_call" | custom-call | tf_op jit(solution)/shard_map/finish/pallas_call | solution.py:366
  (4 shorter events, 0.1 us)
Async XLA Ops:
  2.2 6.5 %collective-permute-start = (bf16[2,128,3584]{2,1,0:T(8,128)(2,1)S(1)}, bf16[2,128,3584]{2,1,0:T(8,128)(2,1)S(1)}, u32[]{:S(2)}, u32[]{:S(2)}) collective-permute-start(bf16[2,128,3584]{2,1,0:T(8,128)(2,1)S(1)} %half.1), channel_id=1, source_target_pairs={{0,1},{1,0},{2,3},{3,2},{4,5},{5,4},{6,7},{7,6},{8,9},{9,8},{10,11... | collective-permute-start | bytes 5505032 | tf_op jit(solution)/shard_map/ppermute | solution.py:34
  7.1 2.2 %copy-start = (bf16[2,128,3584]{2,1,0:T(8,128)(2,1)}, bf16[2,128,3584]{2,1,0:T(8,128)(2,1)S(1)}, u32[]{:S(2)}) copy-start(bf16[2,128,3584]{2,1,0:T(8,128)(2,1)S(1)} %get-tuple-element.8.own_ref) | copy-start | bytes 5505028
  7.1 1.5 %collective-permute-start.1 = (bf16[2,64,256]{2,1,0:T(8,128)(2,1)S(1)}, bf16[2,64,256]{2,1,0:T(8,128)(2,1)S(1)}, u32[]{:S(2)}, u32[]{:S(2)}) collective-permute-start(bf16[2,64,256]{2,1,0:T(8,128)(2,1)S(1)} %get-tuple-element.9.mine_ref), channel_id=1, source_target_pairs={{0,1},{1,0},{2,3},{3,2},{4,5},{5,4},{6,7},{7,6},{8,9},{9,8},{10,11... | collective-permute-start | bytes 196616 | tf_op jit(solution)/shard_map/ppermute | solution.py:34
  49.2 17.8 %copy-start.1 = (bf16[2,128,3584]{2,1,0:T(8,128)(2,1)S(1)}, bf16[2,128,3584]{2,1,0:T(8,128)(2,1)}, u32[]{:S(2)}) copy-start(bf16[2,128,3584]{2,1,0:T(8,128)(2,1)} %copy-done) | copy-start | bytes 5505028
  68.2 6.2 %collective-permute-start.3 = (f32[64,512]{1,0:T(8,128)S(1)}, f32[64,512]{1,0:T(8,128)S(1)}, u32[]{:S(2)}, u32[]{:S(2)}) collective-permute-start(f32[64,512]{1,0:T(8,128)S(1)} %inner.1.refs_1_), channel_id=1, source_target_pairs={{0,1},{1,0},{2,3},{3,2},{4,5},{5,4},{6,7},{7,6},{8,9},{9,8},{10,11... | collective-permute-start | bytes 393224 | tf_op jit(solution)/shard_map/ppermute | solution.py:34
  68.8 3.1 %collective-permute-start.2 = (f32[64,128]{1,0:T(8,128)S(1)}, f32[64,128]{1,0:T(8,128)S(1)}, u32[]{:S(2)}, u32[]{:S(2)}) collective-permute-start(f32[64,128]{1,0:T(8,128)S(1)} %gram.1.mine_ref), channel_id=1, source_target_pairs={{0,1},{1,0},{2,3},{3,2},{4,5},{5,4},{6,7},{7,6},{8,9},{9,8},{10,11... | collective-permute-start | bytes 98312 | tf_op jit(solution)/shard_map/ppermute | solution.py:34
